TPU v7x, 32 devices: a whole 2x2x4 slice. The times are simulated.
32 devices in a mesh: row: 4 (over y, core), col: 8 (over z, x).
Axes of the slice: x: 2, y: 2, z: 4, core: 2. Of those that a mesh axis runs over, the one named last changes fastest.
Arguments:
- objects: float32 [2, 2, 1024, 2048], P(None, None, 'row', 'col'), may hold values from -5 to 5
- probe: float32 [2, 2, 128, 128], replicated, may hold values from -6 to 6
- amplitudes: bfloat16 [4, 8, 6, 128, 128], P('row', 'col'), may hold values from 0.29882812 to 3
- owners: int32 [4, 8, 6], P('row', 'col'), may hold values from 0 to 7, as said below
- off_rows: int32 [4, 8, 6], P('row', 'col'), may hold values from 0 to 256
- off_cols: int32 [4, 8, 6], P('row', 'col'), may hold values from 0 to 256
Outputs:
- gradient: float32 [2, 2, 1024, 2048], P(None, None, 'row', 'col')
Inputs may be any that keep to these rules, and one draw needn't show every extreme that they name: Each device's 6 positions go to owners of its own tile row whose tile column is the device's own plus one of -3, -2, -1, 1, 2, 3, 4, taken modulo 8; at most 2 of them to one owner, exactly 2 to one owner from some device of every tile row. Over all devices of a tile row, one owner receives exactly 12 positions and every other owner at most 7.
All inputs are finite; a program needn't handle non-finite values.
Results may differ from a plain program's by a relative error of at most 0.009.
Values may be sent and summed in bfloat16 or wider, within the bound.
No kernel may reach another device: no remote copies, remote signals or barrier semaphores. Data moves between devices by JAX's collectives and lax.ppermute only.
A program may use at most 64 MiB of HBM per device.

v0:
```python
import functools
import math

import jax
import jax.numpy as jnp
import numpy as np
from jax import lax
from jax.experimental import pallas as pl
from jax.experimental.pallas import tpu as pltpu
from jax.sharding import PartitionSpec as P

FRESNEL = 24.0
REACH_OFFSETS = (-3, -2, -1, 1, 2, 3, 4)
CAP = 2
LANES = 128
NOTE = 16
FIELDS = 4
VMEM_BYTES = 40 * 1024 * 1024
FULL_BYTES = 60 * 1024 * 1024
MAIN_BYTES = 48 * 1024 * 1024
BATCH = 6
HEAVY = pl.CostEstimate(flops=10**12, bytes_accessed=10**9, transcendentals=10**9)


def make_tables(width):
    idx = np.arange(width)
    angle = (idx[:, None] * idx[None, :] % width).astype(np.float32) * np.float32(2.0 * math.pi / width)
    scale = np.float32(1.0 / math.sqrt(width))
    f_re = np.cos(angle) * scale
    f_im = -np.sin(angle) * scale
    centred = (idx + width // 2) % width - width // 2
    theta = (centred * centred).astype(np.float32) * np.float32(math.pi * FRESNEL / (width * width))
    d_re = np.cos(theta)
    d_im = -np.sin(theta)
    m_re = d_re[:, None] * f_re - d_im[:, None] * f_im
    m_im = d_re[:, None] * f_im + d_im[:, None] * f_re
    k_re = f_re @ m_re + f_im @ m_im
    k_im = f_re @ m_im - f_im @ m_re
    tables = []
    for re, im in ((k_re, k_im), (f_re, f_im)):
        tables.append(np.block([[re, -im], [im, re]]))
        tables.append(np.block([[re, im], [-im, re]]))
    return jnp.asarray(np.stack(tables).astype(jnp.bfloat16))


def row_partners(nrows, ncols, idle):
    first = [((r, c), (r ^ 1, c)) for r in range(nrows) for c in range(ncols)]
    second = []
    for r in range(nrows):
        other = ((r + 1) ^ 1) - 1
        for c in range(ncols):
            second.append(((r, c), (other, c) if 0 <= other < nrows else idle(r, c)))
    return first, second


def col_partners(nrows, ncols):
    first = [((r, c), (r, c ^ 1)) for r in range(nrows) for c in range(ncols)]
    second = []
    for c in range(ncols):
        other = ((c + 1) ^ 1) - 1
        for r in range(nrows):
            second.append(((r, c), (r, other) if 0 <= other < ncols else (r ^ 1, c)))
    return first, second


def meet(at, step, turn, size):
    odd = (at // 2 if step == 2 else at) % 2
    return (at + size + step * (1 - 2 * odd) * (1 - 2 * turn)) % size


def routes(ncols):
    paired = [
        functools.partial(lambda step, turn, at: meet(at, step, turn, ncols), step, turn)
        for step in (1, 2, 3)
        for turn in (0, 1)
    ]
    return paired + [lambda at: (at + 4) % ncols]


def sides(axis, size):
    at = lax.axis_index(axis)
    return at % 2 == 0, (at > 0) & (at < size - 1)


def join_right(even, odd, border):
    low = lax.broadcasted_iota(jnp.int32, (1, LANES), 1) < border
    return jnp.where(low, even, pltpu.roll(odd, border, 1))


def join_left(even, odd, border):
    low = lax.broadcasted_iota(jnp.int32, (1, LANES), 1) < border
    return jnp.where(low, pltpu.roll(even, border, 1), odd)


def pack_kernel(ways, ncols, amps, owners, at_rows, at_cols, obj, *refs):
    side_one, side_two, msgs, tile, held, ints, sem = refs
    count, width = held.shape[:2]
    rows, cols = obj.shape[2:]
    border = width // 2
    copies = [
        pltpu.make_async_copy(ref, ints.at[number], sem.at[number])
        for number, ref in enumerate((owners, at_rows, at_cols))
    ]
    copies.append(pltpu.make_async_copy(obj, tile, sem.at[3]))
    copies.append(pltpu.make_async_copy(amps.at[0, 0], held, sem.at[4]))
    for copy in copies:
        copy.start()
    for copy in copies:
        copy.wait()

    myself = lax.axis_index("col")
    even_col, _ = sides("col", ncols)
    for pair in range(2):
        planes = (tile.at[pair, 0], tile.at[pair, 1])
        left = join_right(*(plane[:, :LANES] for plane in planes), border)
        right = join_left(*(plane[:, cols - LANES :] for plane in planes), border)
        side_one[pair] = jnp.where(even_col, right, left).astype(jnp.bfloat16)
        side_two[pair] = jnp.where(even_col, left, right).astype(jnp.bfloat16)
    lane_id = lax.broadcasted_iota(jnp.int32, (NOTE, LANES), 1)
    for kind, way in enumerate(ways):
        owner = way(myself)
        found = jnp.int32(0)
        slots = [jnp.int32(0)] * CAP
        for j in range(count):
            mine = ints[0, 0, 0, j] == owner
            for slot in range(CAP):
                slots[slot] = jnp.where(mine & (found == slot), j, slots[slot])
            found = found + mine.astype(jnp.int32)
        note = jnp.zeros((NOTE, LANES), jnp.float32)
        for slot in range(CAP):
            j = slots[slot]
            msgs[kind, slot * width : (slot + 1) * width] = held[j]
            live = (found > slot).astype(jnp.int32)
            for field, value in enumerate((ints[1, 0, 0, j], ints[2, 0, 0, j], live)):
                here = lane_id == slot * FIELDS + field
                note = jnp.where(here, value.astype(jnp.float32), note)
        msgs[kind, CAP * width :] = note.astype(jnp.bfloat16)


def rows_kernel(ncols, nrows, came_one, came_two, obj, side, row_one, row_two):
    rows = side.shape[1]
    border = row_two.shape[2]
    blocks = row_two.shape[1] - 1
    even_col, inner = sides("col", ncols)
    even_row, _ = sides("row", nrows)
    for pair in range(2):
        one = came_one[pair].astype(jnp.float32)
        two = jnp.where(inner, came_two[pair].astype(jnp.float32), 0.0)
        near = jnp.where(even_col, one, two)
        far = jnp.where(even_col, two, one)
        side[2 * pair] = join_right(near, far, border).astype(jnp.bfloat16)
        side[2 * pair + 1] = join_left(near, far, border).astype(jnp.bfloat16)
    low = pl.multiple_of(jnp.where(even_row, rows - border, 0), border)
    high = pl.multiple_of(jnp.where(even_row, 0, rows - border), border)
    for message, start in ((row_one, low), (row_two, high)):
        for plane in range(4):
            for block in range(blocks):
                here = obj[plane, pl.ds(start, border), block * LANES : (block + 1) * LANES]
                message[plane, block] = here.astype(jnp.bfloat16)
            message[plane, blocks] = side[plane, pl.ds(start, border), :]


def matmul(first, second):
    return jnp.dot(first, second, preferred_element_type=jnp.float32)


def quarters(field):
    half = field.shape[0] // 2
    return field[:half, :half], field[:half, half:], field[half:, :half], field[half:, half:]


def joined(a, b, c, d):
    return jnp.concatenate(
        [jnp.concatenate([a, b], axis=1), jnp.concatenate([c, d], axis=1)], axis=0
    ).astype(jnp.bfloat16)


def swapped(field):
    a, b, c, d = quarters(field)
    return joined(a, c, b, d)


def after_rows(nrows, rows, border):
    even_row, inner = sides("row", nrows)
    one = pl.multiple_of(jnp.where(even_row, border + rows, 0), border)
    two = pl.multiple_of(jnp.where(even_row, 0, border + rows), border)
    return one, two, inner


def extend_kernel(nrows, obj, side, row_one, row_two, ext):
    rows, cols = obj.shape[1:]
    border = row_one.shape[2]
    blocks = cols // LANES
    after_one, after_two, inner = after_rows(nrows, rows, border)
    for plane in range(4):
        for block in range(blocks):
            ext[plane, block, border : border + rows] = obj[plane, :, block * LANES : (block + 1) * LANES]
        ext[plane, blocks, border : border + rows] = side[plane].astype(jnp.float32)
        for block in range(blocks + 1):
            ext[plane, block, pl.ds(after_one, border), :] = row_one[plane, block].astype(jnp.float32)
            ext[plane, block, pl.ds(after_two, border), :] = jnp.where(
                inner, row_two[plane, block].astype(jnp.float32), 0.0
            )


def main_kernel(batch, ncols, nrows, *refs):
    (given_tables, given_probe, given_msgs, given_ext), refs = refs[:4], refs[4:]
    (grad, out_one, out_two, mid_one, mid_two), refs = refs[:5], refs[5:]
    tables, probe, msgs, ext, notes, notes_s, order, sem = refs
    kinds = msgs.shape[0]
    width = probe.shape[2]
    border = width // 2
    blocks = ext.shape[1] - 1
    rows = ext.shape[2] - 2 * border
    span = (blocks + 1) * LANES

    copies = [
        pltpu.make_async_copy(
            given_msgs.at[:, pl.ds(CAP * width, NOTE)], msgs.at[:, pl.ds(CAP * width, NOTE)], sem.at[0]
        ),
        pltpu.make_async_copy(given_ext, ext, sem.at[5]),
        pltpu.make_async_copy(given_tables, tables, sem.at[1]),
        pltpu.make_async_copy(given_probe, probe, sem.at[2]),
        pltpu.make_async_copy(
            given_msgs.at[:, pl.ds(0, CAP * width)], msgs.at[:, pl.ds(0, CAP * width)], sem.at[3]
        ),
    ]
    for copy in copies:
        copy.start()
    grad[...] = jnp.zeros_like(grad)
    copies[0].wait()
    for kind in range(kinds):
        note = msgs[kind, CAP * width :].astype(jnp.float32).astype(jnp.int32)
        notes[kind : kind + 1] = note[:1]
    copy = pltpu.make_async_copy(notes, notes_s, sem.at[4])
    copy.start()
    copy.wait()
    total = jnp.int32(0)
    for kind in range(kinds):
        for slot in range(CAP):
            order[total] = kind * CAP + slot
            total = total + notes_s[kind, slot * FIELDS + 2]
    for spare in range(batch):
        order[total + spare] = 0

    lane = lax.broadcasted_iota(jnp.int32, (1, LANES), 1)

    def stages(items):
        places = []
        for number in items:
            kind, slot = order[number] // CAP, order[number] % CAP
            row = notes_s[kind, slot * FIELDS]
            col = notes_s[kind, slot * FIELDS + 1]
            start = col + (span - border)
            start = jnp.where(start >= span, start - span, start)
            first = start // LANES
            shift = start % LANES
            second = jnp.where(first == blocks, 0, first + 1)
            places.append((kind, slot, row, first, second, shift))
        windows = []
        for _, _, row, first, second, shift in places:
            window = []
            for plane in range(4):
                a = ext[plane, first, pl.ds(row, width), :]
                b = ext[plane, second, pl.ds(row, width), :]
                both = jnp.where(lane >= shift, a, b)
                window.append(pltpu.roll(both, (LANES - shift) % LANES, 1))
            windows.append(window)
        fields = []
        for window in windows:
            parts = []
            for mode in range(2):
                p_re, p_im = probe[mode, 0], probe[mode, 1]
                parts.append((p_re * window[0] - p_im * window[1], p_re * window[1] + p_im * window[0]))
            fields.append(joined(parts[0][0], parts[1][0], parts[0][1], parts[1][1]))
        fields = [swapped(matmul(tables[0], f)) for f in fields]
        phis = [matmul(f, tables[1]) for f in fields]
        fields = []
        for window, phi in zip(windows, phis):
            a_re, a_im, b_re, b_im = quarters(phi)
            w_re, w_im = window[2], window[3]
            fields.append(
                joined(
                    a_re * w_re - a_im * w_im,
                    b_re * w_re - b_im * w_im,
                    a_re * w_im + a_im * w_re,
                    b_re * w_im + b_im * w_re,
                )
            )
        fields = [swapped(matmul(tables[2], f)) for f in fields]
        fars = [matmul(f, tables[3]) for f in fields]
        fields = []
        for place, far in zip(places, fars):
            a_re, a_im, b_re, b_im = quarters(far)
            inten = a_re * a_re + a_im * a_im + b_re * b_re + b_im * b_im
            kind, slot = place[:2]
            amp = msgs[kind, pl.ds(pl.multiple_of(slot * width, width), width), :].astype(jnp.float32)
            keep = 1.0 - amp * lax.rsqrt(jnp.maximum(inten, 1.0))
            fields.append(joined(a_re * keep, b_re * keep, a_im * keep, b_im * keep))
        fields = [swapped(matmul(tables[3], f)) for f in fields]
        seconds = [matmul(f, tables[2]) for f in fields]
        fields = []
        for window, second in zip(windows, seconds):
            a_re, a_im, b_re, b_im = quarters(second)
            w_re, w_im = window[2], window[3]
            fields.append(
                joined(
                    w_re * a_re + w_im * a_im,
                    w_re * b_re + w_im * b_im,
                    w_re * a_im - w_im * a_re,
                    w_re * b_im - w_im * b_re,
                )
            )
        fields = [swapped(matmul(tables[1], f)) for f in fields]
        firsts = [matmul(f, tables[0]) for f in fields]
        for number, place, phi, one, two in zip(items, places, phis, firsts, seconds):
            _, _, row, first, second, shift = place
            sums = []
            probes = (probe[0, 0], probe[0, 1], probe[1, 0], probe[1, 1])
            for left, right in ((probes, one), (quarters(phi), two)):
                p_re, p_im, q_re, q_im = left
                a_re, a_im, b_re, b_im = quarters(right)
                sums.append(p_re * a_re + p_im * a_im + q_re * b_re + q_im * b_im)
                sums.append(p_re * a_im - p_im * a_re + q_re * b_im - q_im * b_re)
            live = number < total
            for plane in range(4):
                moved = pltpu.roll(sums[plane], shift, 1)
                grad[plane, first, pl.ds(row, width), :] += jnp.where((lane >= shift) & live, moved, 0.0)
                grad[plane, second, pl.ds(row, width), :] += jnp.where((lane < shift) & live, moved, 0.0)

    def visit(step, carry):
        stages([batch * step + item for item in range(batch)])
        return carry

    for copy in copies[1:]:
        copy.wait()
    lax.fori_loop(0, (total + batch - 1) // batch, visit, 0)

    after_one, after_two, _ = after_rows(nrows, rows, border)
    for plane in range(4):
        for block in range(blocks + 1):
            out_one[plane, block] = grad[plane, block, pl.ds(after_one, border), :].astype(jnp.bfloat16)
            out_two[plane, block] = grad[plane, block, pl.ds(after_two, border), :].astype(jnp.bfloat16)
    even_col, _ = sides("col", ncols)
    middle = slice(2 * border, rows)
    for pair in range(2):
        even, odd = grad[2 * pair, blocks, middle], grad[2 * pair + 1, blocks, middle]
        right, left = join_right(even, odd, border), join_left(even, odd, border)
        mid_one[pair] = jnp.where(even_col, right, left).astype(jnp.bfloat16)
        mid_two[pair] = jnp.where(even_col, left, right).astype(jnp.bfloat16)


def sides_kernel(ncols, nrows, grad, came_one, came_two, middle, side_one, side_two):
    blocks = grad.shape[1] - 1
    border = came_one.shape[2]
    rows = grad.shape[2] - 2 * border
    even_col, _ = sides("col", ncols)
    even_row, inner = sides("row", nrows)

    def ends(plane, block):
        one = came_one[plane, block].astype(jnp.float32)
        two = jnp.where(inner, came_two[plane, block].astype(jnp.float32), 0.0)
        top = grad[plane, block, border : 2 * border] + jnp.where(even_row, two, one)
        bottom = grad[plane, block, rows : rows + border] + jnp.where(even_row, one, two)
        return top, bottom

    for pair in range(2):
        for number, (even, odd) in enumerate(zip(ends(2 * pair, blocks), ends(2 * pair + 1, blocks))):
            right, left = join_right(even, odd, border), join_left(even, odd, border)
            span = slice(number * border, (number + 1) * border)
            side_one[pair, span] = jnp.where(even_col, right, left).astype(jnp.bfloat16)
            side_two[pair, span] = jnp.where(even_col, left, right).astype(jnp.bfloat16)
    for plane in range(4):
        for block in range(blocks):
            span = slice(block * LANES, (block + 1) * LANES)
            top, bottom = ends(plane, block)
            middle[plane, :border, span] = top
            middle[plane, border : rows - border, span] = grad[plane, block, 2 * border : rows]
            middle[plane, rows - border :, span] = bottom


def final_kernel(ncols, border, middle, mid_one, mid_two, end_one, end_two, out):
    rows, cols = middle.shape[1:]
    low = lax.broadcasted_iota(jnp.int32, (1, LANES), 1) < border
    even_col, inner = sides("col", ncols)
    parts = (
        (slice(0, border), end_one, end_two, slice(0, border)),
        (slice(border, rows - border), mid_one, mid_two, slice(0, rows - 2 * border)),
        (slice(rows - border, rows), end_one, end_two, slice(border, 2 * border)),
    )
    for span, came_one, came_two, source in parts:
        for pair in range(2):
            one = came_one[pair, source].astype(jnp.float32)
            two = jnp.where(inner, came_two[pair, source].astype(jnp.float32), 0.0)
            near = jnp.where(even_col, two, one)
            far = jnp.where(even_col, one, two)
            even, odd = 2 * pair, 2 * pair + 1
            for plane, first, last in (
                (even, near, pltpu.roll(far, border, 1)),
                (odd, pltpu.roll(near, border, 1), far),
            ):
                add_first = jnp.where(low, first, 0.0)
                add_last = jnp.where(low, 0.0, last)
                if cols == LANES:
                    out[plane, span] = middle[plane, span] + add_first + add_last
                    continue
                out[plane, span, :LANES] = middle[plane, span, :LANES] + add_first
                if cols > 2 * LANES:
                    out[plane, span, LANES : cols - LANES] = middle[plane, span, LANES : cols - LANES]
                out[plane, span, cols - LANES :] = middle[plane, span, cols - LANES :] + add_last


def local(ncols, nrows, objects, probe, amplitudes, owners, off_rows, off_cols):
    width = amplitudes.shape[-1]
    border = width // 2
    count = amplitudes.shape[2]
    rows, cols = objects.shape[2:]
    blocks = cols // LANES
    obj = objects.reshape(4, rows, cols)
    vmem = pl.BlockSpec(memory_space=pltpu.VMEM)
    anywhere = pl.BlockSpec(memory_space=pl.ANY)
    bf16 = functools.partial(jax.ShapeDtypeStruct, dtype=jnp.bfloat16)
    f32 = functools.partial(jax.ShapeDtypeStruct, dtype=jnp.float32)

    def kernel(body, ins, outs, name, scratch=(), limit=VMEM_BYTES, cost=None):
        return pl.pallas_call(
            body,
            out_shape=outs,
            in_specs=ins if isinstance(ins, list) else [vmem] * ins,
            out_specs=[vmem] * len(outs),
            scratch_shapes=list(scratch),
            compiler_params=pltpu.CompilerParams(vmem_limit_bytes=limit),
            cost_estimate=cost,
            name=name,
        )

    def across(array, way):
        return lax.ppermute(array, "col", [(i, way(i)) for i in range(ncols)])

    def swap(array, pairs):
        flat = [(a * ncols + b, c * ncols + d) for (a, b), (c, d) in pairs]
        return lax.ppermute(array, ("row", "col"), flat)

    row_one, row_two = row_partners(nrows, ncols, lambda r, c: (nrows - 1 - r, c))
    _, row_back = row_partners(nrows, ncols, lambda r, c: (r, c ^ 2))
    col_one, col_two = col_partners(nrows, ncols)
    if ncols == 8:
        ways = [functools.partial(lambda to, at: to, to) for to in range(ncols)]
    else:
        ways = routes(ncols)
    kinds = len(ways)
    line_shape = bf16((4, blocks + 1, border, LANES))
    side_shape = bf16((2, rows, LANES))

    side_one, side_two, msgs = kernel(
        functools.partial(pack_kernel, ways, ncols),
        [anywhere] * 5,
        [side_shape] * 2 + [bf16((kinds, CAP * width + NOTE, LANES))],
        "pack",
        [
            pltpu.VMEM(objects.shape, jnp.float32),
            pltpu.VMEM((count, width, width), jnp.bfloat16),
            pltpu.SMEM((3,) + owners.shape, jnp.int32),
            pltpu.SemaphoreType.DMA((5,)),
        ],
        FULL_BYTES,
    )(amplitudes, owners, off_rows, off_cols, objects)
    came_one, came_two = swap(side_one, col_one), swap(side_two, col_two)
    if ncols == 8:
        msgs = lax.all_to_all(msgs, "col", 0, 0)
    else:
        msgs = jnp.stack([across(msgs[kind], way) for kind, way in enumerate(ways)])
    side, line_one, line_two = kernel(
        functools.partial(rows_kernel, ncols, nrows),
        3,
        [bf16((4, rows, LANES))] + [line_shape] * 2,
        "rows",
        cost=HEAVY,
    )(came_one, came_two, obj)
    line_one, line_two = swap(line_one, row_one), swap(line_two, row_two)

    whole = f32((4, blocks + 1, rows + 2 * border, LANES))
    (ext,) = kernel(functools.partial(extend_kernel, nrows), 4, [whole], "extend")(
        obj, side, line_one, line_two
    )
    tables = make_tables(width)
    grad, line_one, line_two, mid_one, mid_two = kernel(
        functools.partial(main_kernel, BATCH, ncols, nrows),
        [anywhere] * 4,
        [whole] + [line_shape] * 2 + [bf16((2, rows - 2 * border, LANES))] * 2,
        "gradients",
        [
            pltpu.VMEM(tables.shape, jnp.bfloat16),
            pltpu.VMEM(probe.shape, jnp.float32),
            pltpu.VMEM(msgs.shape, jnp.bfloat16),
            pltpu.VMEM(whole.shape, jnp.float32),
            pltpu.VMEM((8, LANES), jnp.int32),
            pltpu.SMEM((8, LANES), jnp.int32),
            pltpu.SMEM((kinds * CAP + BATCH,), jnp.int32),
            pltpu.SemaphoreType.DMA((6,)),
        ],
        MAIN_BYTES,
    )(tables, probe, msgs, ext)

    line_two, line_one = swap(line_two, row_back), swap(line_one, row_one)
    mid_one, mid_two = swap(mid_one, col_one), swap(mid_two, col_two)
    middle, end_one, end_two = kernel(
        functools.partial(sides_kernel, ncols, nrows),
        3,
        [f32((4, rows, cols))] + [bf16((2, 2 * border, LANES))] * 2,
        "sides",
    )(grad, line_one, line_two)
    end_one, end_two = swap(end_one, col_one), swap(end_two, col_two)
    (out,) = kernel(
        functools.partial(final_kernel, ncols, border), 5, [f32((4, rows, cols))], "final"
    )(middle, mid_one, mid_two, end_one, end_two)
    return out.reshape(objects.shape)


def solution(mesh):
    placed = (
        P(None, None, "row", "col"),
        P(),
        P("row", "col", None, None, None),
        P("row", "col", None),
        P("row", "col", None),
        P("row", "col", None),
    )
    return jax.shard_map(
        functools.partial(local, mesh.shape["col"], mesh.shape["row"]),
        mesh=mesh,
        in_specs=placed,
        out_specs=P(None, None, "row", "col"),
        check_vma=False,
    )
```

profile of v0, /device:TPU:0, one launch (start us, length us, event | category | flops | bytes accessed | tf_op | source)
XLA Modules:
  0.0 43.8 jit_solution(47724559911555407)
XLA Ops:
  0.0 0.0 copy-start.1
  0.0 2.5 %pack.1 = (bf16[2,256,128]{2,1,0:T(8,128)(2,1)}, bf16[2,256,128]{2,1,0:T(8,128)(2,1)}, bf16[8,272,128]{2,1,0:T(8,128)(2,1)}) custom-call(bf16[1,1,6,128,128]{4,3,2,1,0:T(8,128)(2,1)} %amps.1, s32[1,1,6]{2,1,0:T(1,128)} %owners.1, s32[1,1,6]{2,1,0:T(1,128)} %at_rows.1, s32[1,1,6]{2,1,0:T(1,128)} %at_cols.1, f32[2,2,256,256]{3,2,1,0:T(8,128)} %obj.1), custom_call_target="tpu_custom_call" | custom-call | tf_op jit(solution)/shard_map/pack/pallas_call | solution.py:455
  2.5 3.0 %collective-permute-start = (bf16[2,256,128]{2,1,0:T(8,128)(2,1)}, bf16[2,256,128]{2,1,0:T(8,128)(2,1)S(1)}, u32[]{:S(2)}, u32[]{:S(2)}) collective-permute-start(bf16[2,256,128]{2,1,0:T(8,128)(2,1)} %get-tuple-element.20), channel_id=1, source_target_pairs={{0,1},{1,0},{2,3},{3,2},{4,5},{5,4},{6,7},{7,6},{8,9},{9,8},{10,11... | collective-permute-start | bytes 393224 | tf_op jit(solution)/shard_map/ppermute | solution.py:442
  5.5 0.0 collective-permute-start.1
  5.5 6.3 %all-to-all-start = ((bf16[8,272,128]{2,1,0:T(8,128)(2,1)}), bf16[8,272,128]{2,1,0:T(8,128)(2,1)}, u32[]{:S(2)}, u32[]{:S(2)}) async-start(bf16[8,272,128]{2,1,0:T(8,128)(2,1)} %get-tuple-element.19), calls=%async_computation | async-start | bytes 1114112 | tf_op jit(solution)/shard_map/all_to_all | solution.py:470
  11.9 0.0 collective-permute-done.came_one
  11.9 0.0 collective-permute-done.1.came_two
  11.9 0.0 copy-done.1
  11.9 0.2 rows.1
  12.1 0.0 copy-start.2
  12.1 0.0 copy-start.3
  12.1 0.1 collective-permute-start.2
  12.2 1.6 %collective-permute-start.3 = (bf16[4,3,64,128]{3,2,1,0:T(8,128)(2,1)S(1)}, bf16[4,3,64,128]{3,2,1,0:T(8,128)(2,1)S(1)}, u32[]{:S(2)}, u32[]{:S(2)}) collective-permute-start(bf16[4,3,64,128]{3,2,1,0:T(8,128)(2,1)S(1)} %get-tuple-element.24), channel_id=1, source_target_pairs={{0,24},{1,25},{2,26},{3,27},{4,28},{5,29},{6,30},{7,31},{8,16},{9,... | collective-permute-start | bytes 589832 | tf_op jit(solution)/shard_map/ppermute | solution.py:442
  13.8 0.0 collective-permute-done.2.row_one
  13.8 5.1 %collective-permute-done.3.row_two = bf16[4,3,64,128]{3,2,1,0:T(8,128)(2,1)S(1)} collective-permute-done((bf16[4,3,64,128]{3,2,1,0:T(8,128)(2,1)S(1)}, bf16[4,3,64,128]{3,2,1,0:T(8,128)(2,1)S(1)}, u32[]{:S(2)}, u32[]{:S(2)}) %collective-permute-start.3) | collective-permute-done | bytes 196640 | tf_op jit(solution)/shard_map/ppermute | solution.py:442
  18.9 0.2 extend.1.refs_3_
  19.1 0.0 copy-start
  19.1 1.4 %copy-done = f32[4,3,384,128]{3,2,1,0:T(8,128)} copy-done((f32[4,3,384,128]{3,2,1,0:T(8,128)}, f32[4,3,384,128]{3,2,1,0:T(8,128)S(1)}, u32[]{:S(2)}) %copy-start) | copy-done | bytes 2359320
  20.5 6.2 %all-to-all-done.refs_2_ = bf16[8,272,128]{2,1,0:T(8,128)(2,1)} async-done(((bf16[8,272,128]{2,1,0:T(8,128)(2,1)}), bf16[8,272,128]{2,1,0:T(8,128)(2,1)}, u32[]{:S(2)}, u32[]{:S(2)}) %all-to-all-start) | async-done | bytes 557088 | tf_op jit(solution)/shard_map/all_to_all | solution.py:470
  26.6 0.0 copy-done.2
  26.6 0.0 copy-done.3
  26.6 4.7 %gradients.1 = (f32[4,3,384,128]{3,2,1,0:T(8,128)S(1)}, bf16[4,3,64,128]{3,2,1,0:T(8,128)(2,1)S(1)}, bf16[4,3,64,128]{3,2,1,0:T(8,128)(2,1)S(1)}, bf16[2,128,128...) custom-call(bf16[4,256,256]{2,1,0:T(8,128)(2,1)S(1)} %copy-done.2, f32[2,2,128,128]{3,2,1,0:T(8,128)S(1)} %copy-done.3, ...), custom_call_target="tpu_custom_call" | custom-call | tf_op jit(solution)/shard_map/gradients/pallas_call | solution.py:487
  31.4 0.1 collective-permute-start.4
  31.5 0.7 %collective-permute-start.5 = (bf16[4,3,64,128]{3,2,1,0:T(8,128)(2,1)S(1)}, bf16[4,3,64,128]{3,2,1,0:T(8,128)(2,1)S(1)}, u32[]{:S(2)}, u32[]{:S(2)}) collective-permute-start(bf16[4,3,64,128]{3,2,1,0:T(8,128)(2,1)S(1)} %get-tuple-element.27), channel_id=1, source_target_pairs={{0,2},{1,3},{2,0},{3,1},{4,6},{5,7},{6,4},{7,5},{8,16},{9,17},{10,... | collective-permute-start | bytes 589832 | tf_op jit(solution)/shard_map/ppermute | solution.py:442
  32.2 0.9 %collective-permute-start.6 = (bf16[2,128,128]{2,1,0:T(8,128)(2,1)S(1)}, bf16[2,128,128]{2,1,0:T(8,128)(2,1)S(1)}, u32[]{:S(2)}, u32[]{:S(2)}) collective-permute-start(bf16[2,128,128]{2,1,0:T(8,128)(2,1)S(1)} %get-tuple-element.29), channel_id=1, source_target_pairs={{0,1},{1,0},{2,3},{3,2},{4,5},{5,4},{6,7},{7,6},{8,9},{9,8},{10,11... | collective-permute-start | bytes 196616 | tf_op jit(solution)/shard_map/ppermute | solution.py:442
  33.0 2.8 %collective-permute-start.7 = (bf16[2,128,128]{2,1,0:T(8,128)(2,1)S(1)}, bf16[2,128,128]{2,1,0:T(8,128)(2,1)S(1)}, u32[]{:S(2)}, u32[]{:S(2)}) collective-permute-start(bf16[2,128,128]{2,1,0:T(8,128)(2,1)S(1)} %get-tuple-element.30), channel_id=1, source_target_pairs={{0,8},{8,0},{16,24},{24,16},{1,2},{9,10},{17,18},{25,26},{2,1},{10... | collective-permute-start | bytes 196616 | tf_op jit(solution)/shard_map/ppermute | solution.py:442
  35.8 0.0 collective-permute-done.4.came_one
  35.8 1.4 %collective-permute-done.5.came_two = bf16[4,3,64,128]{3,2,1,0:T(8,128)(2,1)S(1)} collective-permute-done((bf16[4,3,64,128]{3,2,1,0:T(8,128)(2,1)S(1)}, bf16[4,3,64,128]{3,2,1,0:T(8,128)(2,1)S(1)}, u32[]{:S(2)}, u32[]{:S(2)}) %collective-permute-start.5) | collective-permute-done | bytes 196640 | tf_op jit(solution)/shard_map/ppermute | solution.py:442
  37.2 0.2 sides.1
  37.4 1.5 %collective-permute-start.8 = (bf16[2,128,128]{2,1,0:T(8,128)(2,1)S(1)}, bf16[2,128,128]{2,1,0:T(8,128)(2,1)S(1)}, u32[]{:S(2)}, u32[]{:S(2)}) collective-permute-start(bf16[2,128,128]{2,1,0:T(8,128)(2,1)S(1)} %get-tuple-element.31), channel_id=1, source_target_pairs={{0,1},{1,0},{2,3},{3,2},{4,5},{5,4},{6,7},{7,6},{8,9},{9,8},{10,11... | collective-permute-start | bytes 196616 | tf_op jit(solution)/shard_map/ppermute | solution.py:442
  38.9 0.6 %collective-permute-start.9 = (bf16[2,128,128]{2,1,0:T(8,128)(2,1)S(1)}, bf16[2,128,128]{2,1,0:T(8,128)(2,1)S(1)}, u32[]{:S(2)}, u32[]{:S(2)}) collective-permute-start(bf16[2,128,128]{2,1,0:T(8,128)(2,1)S(1)} %get-tuple-element.32), channel_id=1, source_target_pairs={{0,8},{8,0},{16,24},{24,16},{1,2},{9,10},{17,18},{25,26},{2,1},{10... | collective-permute-start | bytes 196616 | tf_op jit(solution)/shard_map/ppermute | solution.py:442
  39.5 0.0 collective-permute-done.6.mid_one
  39.5 0.0 collective-permute-done.7.mid_two
  39.5 3.2 %collective-permute-done.8.end_one = bf16[2,128,128]{2,1,0:T(8,128)(2,1)S(1)} collective-permute-done((bf16[2,128,128]{2,1,0:T(8,128)(2,1)S(1)}, bf16[2,128,128]{2,1,0:T(8,128)(2,1)S(1)}, u32[]{:S(2)}, u32[]{:S(2)}) %collective-permute-start.8) | collective-permute-done | bytes 65568 | tf_op jit(solution)/shard_map/ppermute | solution.py:442
  42.7 0.0 collective-permute-done.9.end_two
  42.7 1.1 %final.1 = f32[4,256,256]{2,1,0:T(8,128)} custom-call(f32[4,256,256]{2,1,0:T(8,128)S(1)} %get-tuple-element.28.middle, bf16[2,128,128]{2,1,0:T(8,128)(2,1)S(1)} %collective-permute-done.6.mid_one, bf16[2,128,128]{2,1,0:T(8,128)(2,1)S(1)} %collective-permute-done.7.mid_two, bf16[2,128,128]{2,1,0:T(8,128)(2,1)S(1)} %collective-permute-done.8.end_one, ...), custom_call_target="tpu_custom_call" | custom-call | tf_op jit(solution)/shard_map/final/pallas_call | solution.py:514
Async XLA Ops:
  0.0 11.9 %copy-start.1 = (f32[2,2,256,256]{3,2,1,0:T(8,128)S(1)}, f32[2,2,256,256]{3,2,1,0:T(8,128)}, u32[]{:S(2)}) copy-start(f32[2,2,256,256]{3,2,1,0:T(8,128)} %obj.1) | copy-start | bytes 3145732
  2.5 9.3 %collective-permute-start = (bf16[2,256,128]{2,1,0:T(8,128)(2,1)}, bf16[2,256,128]{2,1,0:T(8,128)(2,1)S(1)}, u32[]{:S(2)}, u32[]{:S(2)}) collective-permute-start(bf16[2,256,128]{2,1,0:T(8,128)(2,1)} %get-tuple-element.20), channel_id=1, source_target_pairs={{0,1},{1,0},{2,3},{3,2},{4,5},{5,4},{6,7},{7,6},{8,9},{9,8},{10,11... | collective-permute-start | bytes 393224 | tf_op jit(solution)/shard_map/ppermute | solution.py:442
  5.5 6.3 %collective-permute-start.1 = (bf16[2,256,128]{2,1,0:T(8,128)(2,1)}, bf16[2,256,128]{2,1,0:T(8,128)(2,1)S(1)}, u32[]{:S(2)}, u32[]{:S(2)}) collective-permute-start(bf16[2,256,128]{2,1,0:T(8,128)(2,1)} %get-tuple-element.21), channel_id=1, source_target_pairs={{0,8},{8,0},{16,24},{24,16},{1,2},{9,10},{17,18},{25,26},{2,1},{10... | collective-permute-start | bytes 393224 | tf_op jit(solution)/shard_map/ppermute | solution.py:442
  5.5 21.1 %all-to-all-start = ((bf16[8,272,128]{2,1,0:T(8,128)(2,1)}), bf16[8,272,128]{2,1,0:T(8,128)(2,1)}, u32[]{:S(2)}, u32[]{:S(2)}) async-start(bf16[8,272,128]{2,1,0:T(8,128)(2,1)} %get-tuple-element.19), calls=%async_computation | async-start | bytes 1114112 | tf_op jit(solution)/shard_map/all_to_all | solution.py:470
  12.1 14.6 %copy-start.2 = (bf16[4,256,256]{2,1,0:T(8,128)(2,1)S(1)}, bf16[4,256,256]{2,1,0:T(8,128)(2,1)}, u32[]{:S(2)}) copy-start(bf16[4,256,256]{2,1,0:T(8,128)(2,1)} %constant.2.clone.refs_0_) | copy-start | bytes 1572868
  12.1 14.5 %copy-start.3 = (f32[2,2,128,128]{3,2,1,0:T(8,128)S(1)}, f32[2,2,128,128]{3,2,1,0:T(8,128)}, u32[]{:S(2)}) copy-start(f32[2,2,128,128]{3,2,1,0:T(8,128)} %refs_1_.1) | copy-start | bytes 786436
  12.1 1.7 %collective-permute-start.2 = (bf16[4,3,64,128]{3,2,1,0:T(8,128)(2,1)S(1)}, bf16[4,3,64,128]{3,2,1,0:T(8,128)(2,1)S(1)}, u32[]{:S(2)}, u32[]{:S(2)}) collective-permute-start(bf16[4,3,64,128]{3,2,1,0:T(8,128)(2,1)S(1)} %get-tuple-element.23), channel_id=1, source_target_pairs={{0,8},{1,9},{2,10},{3,11},{4,12},{5,13},{6,14},{7,15},{8,0},{9,1},... | collective-permute-start | bytes 589832 | tf_op jit(solution)/shard_map/ppermute | solution.py:442
  12.2 6.7 %collective-permute-start.3 = (bf16[4,3,64,128]{3,2,1,0:T(8,128)(2,1)S(1)}, bf16[4,3,64,128]{3,2,1,0:T(8,128)(2,1)S(1)}, u32[]{:S(2)}, u32[]{:S(2)}) collective-permute-start(bf16[4,3,64,128]{3,2,1,0:T(8,128)(2,1)S(1)} %get-tuple-element.24), channel_id=1, source_target_pairs={{0,24},{1,25},{2,26},{3,27},{4,28},{5,29},{6,30},{7,31},{8,16},{9,... | collective-permute-start | bytes 589832 | tf_op jit(solution)/shard_map/ppermute | solution.py:442
  19.1 1.4 %copy-start = (f32[4,3,384,128]{3,2,1,0:T(8,128)}, f32[4,3,384,128]{3,2,1,0:T(8,128)S(1)}, u32[]{:S(2)}) copy-start(f32[4,3,384,128]{3,2,1,0:T(8,128)S(1)} %extend.1.refs_3_) | copy-start | bytes 7077892
  31.4 4.4 %collective-permute-start.4 = (bf16[4,3,64,128]{3,2,1,0:T(8,128)(2,1)S(1)}, bf16[4,3,64,128]{3,2,1,0:T(8,128)(2,1)S(1)}, u32[]{:S(2)}, u32[]{:S(2)}) collective-permute-start(bf16[4,3,64,128]{3,2,1,0:T(8,128)(2,1)S(1)} %get-tuple-element.26), channel_id=1, source_target_pairs={{0,8},{1,9},{2,10},{3,11},{4,12},{5,13},{6,14},{7,15},{8,0},{9,1},... | collective-permute-start | bytes 589832 | tf_op jit(solution)/shard_map/ppermute | solution.py:442
  31.5 5.7 %collective-permute-start.5 = (bf16[4,3,64,128]{3,2,1,0:T(8,128)(2,1)S(1)}, bf16[4,3,64,128]{3,2,1,0:T(8,128)(2,1)S(1)}, u32[]{:S(2)}, u32[]{:S(2)}) collective-permute-start(bf16[4,3,64,128]{3,2,1,0:T(8,128)(2,1)S(1)} %get-tuple-element.27), channel_id=1, source_target_pairs={{0,2},{1,3},{2,0},{3,1},{4,6},{5,7},{6,4},{7,5},{8,16},{9,17},{10,... | collective-permute-start | bytes 589832 | tf_op jit(solution)/shard_map/ppermute | solution.py:442
  32.2 7.3 %collective-permute-start.6 = (bf16[2,128,128]{2,1,0:T(8,128)(2,1)S(1)}, bf16[2,128,128]{2,1,0:T(8,128)(2,1)S(1)}, u32[]{:S(2)}, u32[]{:S(2)}) collective-permute-start(bf16[2,128,128]{2,1,0:T(8,128)(2,1)S(1)} %get-tuple-element.29), channel_id=1, source_target_pairs={{0,1},{1,0},{2,3},{3,2},{4,5},{5,4},{6,7},{7,6},{8,9},{9,8},{10,11... | collective-permute-start | bytes 196616 | tf_op jit(solution)/shard_map/ppermute | solution.py:442
  33.0 6.4 %collective-permute-start.7 = (bf16[2,128,128]{2,1,0:T(8,128)(2,1)S(1)}, bf16[2,128,128]{2,1,0:T(8,128)(2,1)S(1)}, u32[]{:S(2)}, u32[]{:S(2)}) collective-permute-start(bf16[2,128,128]{2,1,0:T(8,128)(2,1)S(1)} %get-tuple-element.30), channel_id=1, source_target_pairs={{0,8},{8,0},{16,24},{24,16},{1,2},{9,10},{17,18},{25,26},{2,1},{10... | collective-permute-start | bytes 196616 | tf_op jit(solution)/shard_map/ppermute | solution.py:442
  37.4 5.3 %collective-permute-start.8 = (bf16[2,128,128]{2,1,0:T(8,128)(2,1)S(1)}, bf16[2,128,128]{2,1,0:T(8,128)(2,1)S(1)}, u32[]{:S(2)}, u32[]{:S(2)}) collective-permute-start(bf16[2,128,128]{2,1,0:T(8,128)(2,1)S(1)} %get-tuple-element.31), channel_id=1, source_target_pairs={{0,1},{1,0},{2,3},{3,2},{4,5},{5,4},{6,7},{7,6},{8,9},{9,8},{10,11... | collective-permute-start | bytes 196616 | tf_op jit(solution)/shard_map/ppermute | solution.py:442
  38.9 3.8 %collective-permute-start.9 = (bf16[2,128,128]{2,1,0:T(8,128)(2,1)S(1)}, bf16[2,128,128]{2,1,0:T(8,128)(2,1)S(1)}, u32[]{:S(2)}, u32[]{:S(2)}) collective-permute-start(bf16[2,128,128]{2,1,0:T(8,128)(2,1)S(1)} %get-tuple-element.32), channel_id=1, source_target_pairs={{0,8},{8,0},{16,24},{24,16},{1,2},{9,10},{17,18},{25,26},{2,1},{10... | collective-permute-start | bytes 196616 | tf_op jit(solution)/shard_map/ppermute | solution.py:442
where the time goes:
time: 44.4 us; the launch traced here: 43.8 us
  starting transfers between devices  17.5 us (39%)
  waiting for transfers between devices  15.9 us (36%)
  Pallas kernels  8.91 us (20%)
  local copies, waits for them, and re-layouts  1.43 us (3%)
    ppermute x10, starting transfers between devices, swap(): return lax.ppermute(array, ('row', 'col'), flat)  11.2 us
    ppermute x10, waiting for transfers between devices, swap(): return lax.ppermute(array, ('row', 'col'), flat)  9.69 us
    all_to_all x1, starting transfers between devices, local(): msgs = lax.all_to_all(msgs, 'col', 0, 0)  6.34 us
    all_to_all x1, waiting for transfers between devices, local(): msgs = lax.all_to_all(msgs, 'col', 0, 0)  6.16 us
    pallas_call x1, Pallas kernels, local(): kernel(functools.partial(main_kernel, BATCH, ncols, nrows), [anywhere] *...  4.74 us
    pallas_call x1, Pallas kernels, local(): kernel(functools.partial(pack_kernel, ways, ncols), [anywhere] * 5, [side...  2.51 us
    unnamed x8, local copies, waits for them, and re-layouts  1.43 us
    pallas_call x1, Pallas kernels, local(): kernel(functools.partial(final_kernel, ncols, border), 5, [f32((4, rows,...  1.13 us
  transfers between devices with their start and end apart: 11, of which 4 were waited for; matrix products, arithmetic and copies ran while one was open for 0% of the time, Pallas kernels for 1%

commit v1 on v0

--- a/solution.py
+++ b/solution.py
@@ -93,30 +93,24 @@
 
 
 def pack_kernel(ways, ncols, amps, owners, at_rows, at_cols, obj, *refs):
-    side_one, side_two, msgs, tile, held, ints, sem = refs
-    count, width = held.shape[:2]
+    side_one, side_two, msgs, tile, packed, held, chosen, ints, sem, sent = refs
+    count, width = amps.shape[2:4]
     rows, cols = obj.shape[2:]
     border = width // 2
-    copies = [
+    small = [
         pltpu.make_async_copy(ref, ints.at[number], sem.at[number])
         for number, ref in enumerate((owners, at_rows, at_cols))
     ]
-    copies.append(pltpu.make_async_copy(obj, tile, sem.at[3]))
-    copies.append(pltpu.make_async_copy(amps.at[0, 0], held, sem.at[4]))
-    for copy in copies:
+    tiles = [pltpu.make_async_copy(obj.at[pair], tile.at[pair], sem.at[3 + pair]) for pair in range(2)]
+    patterns = pltpu.make_async_copy(amps.at[0, 0], held, sem.at[5])
+    for copy in small + [patterns] + tiles:
         copy.start()
-    for copy in copies:
+    for copy in small + [patterns]:
         copy.wait()
 
     myself = lax.axis_index("col")
-    even_col, _ = sides("col", ncols)
-    for pair in range(2):
-        planes = (tile.at[pair, 0], tile.at[pair, 1])
-        left = join_right(*(plane[:, :LANES] for plane in planes), border)
-        right = join_left(*(plane[:, cols - LANES :] for plane in planes), border)
-        side_one[pair] = jnp.where(even_col, right, left).astype(jnp.bfloat16)
-        side_two[pair] = jnp.where(even_col, left, right).astype(jnp.bfloat16)
     lane_id = lax.broadcasted_iota(jnp.int32, (NOTE, LANES), 1)
+    copies = []
     for kind, way in enumerate(ways):
         owner = way(myself)
         found = jnp.int32(0)
@@ -129,12 +123,29 @@
         note = jnp.zeros((NOTE, LANES), jnp.float32)
         for slot in range(CAP):
             j = slots[slot]
-            msgs[kind, slot * width : (slot + 1) * width] = held[j]
+            chosen[kind, slot * width : (slot + 1) * width] = held[j]
             live = (found > slot).astype(jnp.int32)
             for field, value in enumerate((ints[1, 0, 0, j], ints[2, 0, 0, j], live)):
                 here = lane_id == slot * FIELDS + field
                 note = jnp.where(here, value.astype(jnp.float32), note)
-        msgs[kind, CAP * width :] = note.astype(jnp.bfloat16)
+        chosen[kind, CAP * width :] = note.astype(jnp.bfloat16)
+        copies.append(pltpu.make_async_copy(chosen.at[kind], msgs.at[kind], sent.at[kind]))
+        copies[-1].start()
+
+    even_col, _ = sides("col", ncols)
+    for pair in range(2):
+        tiles[pair].wait()
+        planes = (tile.at[pair, 0], tile.at[pair, 1])
+        left = join_right(*(plane[:, :LANES] for plane in planes), border)
+        right = join_left(*(plane[:, cols - LANES :] for plane in planes), border)
+        packed[0, pair] = jnp.where(even_col, right, left).astype(jnp.bfloat16)
+        packed[1, pair] = jnp.where(even_col, left, right).astype(jnp.bfloat16)
+        for number, side in enumerate((side_one, side_two)):
+            at = sem.at[6 + 2 * pair + number]
+            copies.append(pltpu.make_async_copy(packed.at[number, pair], side.at[pair], at))
+            copies[-1].start()
+    for copy in copies:
+        copy.wait()
 
 
 def rows_kernel(ncols, nrows, came_one, came_two, obj, side, row_one, row_two):
@@ -164,6 +175,12 @@
     return jnp.dot(first, second, preferred_element_type=jnp.float32)
 
 
+def each_times(fields, table):
+    size = fields[0].shape[0]
+    whole = matmul(jnp.concatenate(fields, axis=0), table)
+    return [whole[at : at + size] for at in range(0, whole.shape[0], size)]
+
+
 def quarters(field):
     half = field.shape[0] // 2
     return field[:half, :half], field[:half, half:], field[half:, :half], field[half:, half:]
@@ -205,7 +222,7 @@
 
 def main_kernel(batch, ncols, nrows, *refs):
     (given_tables, given_probe, given_msgs, given_ext), refs = refs[:4], refs[4:]
-    (grad, out_one, out_two, mid_one, mid_two), refs = refs[:5], refs[5:]
+    (grad, out_one, out_two, corner_two, mid_one, mid_two), refs = refs[:6], refs[6:]
     tables, probe, msgs, ext, notes, notes_s, order, sem = refs
     kinds = msgs.shape[0]
     width = probe.shape[2]
@@ -274,7 +291,7 @@
                 parts.append((p_re * window[0] - p_im * window[1], p_re * window[1] + p_im * window[0]))
             fields.append(joined(parts[0][0], parts[1][0], parts[0][1], parts[1][1]))
         fields = [swapped(matmul(tables[0], f)) for f in fields]
-        phis = [matmul(f, tables[1]) for f in fields]
+        phis = each_times(fields, tables[1])
         fields = []
         for window, phi in zip(windows, phis):
             a_re, a_im, b_re, b_im = quarters(phi)
@@ -288,7 +305,7 @@
                 )
             )
         fields = [swapped(matmul(tables[2], f)) for f in fields]
-        fars = [matmul(f, tables[3]) for f in fields]
+        fars = each_times(fields, tables[3])
         fields = []
         for place, far in zip(places, fars):
             a_re, a_im, b_re, b_im = quarters(far)
@@ -298,7 +315,7 @@
             keep = 1.0 - amp * lax.rsqrt(jnp.maximum(inten, 1.0))
             fields.append(joined(a_re * keep, b_re * keep, a_im * keep, b_im * keep))
         fields = [swapped(matmul(tables[3], f)) for f in fields]
-        seconds = [matmul(f, tables[2]) for f in fields]
+        seconds = each_times(fields, tables[2])
         fields = []
         for window, second in zip(windows, seconds):
             a_re, a_im, b_re, b_im = quarters(second)
@@ -312,7 +329,7 @@
                 )
             )
         fields = [swapped(matmul(tables[1], f)) for f in fields]
-        firsts = [matmul(f, tables[0]) for f in fields]
+        firsts = each_times(fields, tables[0])
         for number, place, phi, one, two in zip(items, places, phis, firsts, seconds):
             _, _, row, first, second, shift = place
             sums = []
@@ -340,7 +357,11 @@
     for plane in range(4):
         for block in range(blocks + 1):
             out_one[plane, block] = grad[plane, block, pl.ds(after_one, border), :].astype(jnp.bfloat16)
-            out_two[plane, block] = grad[plane, block, pl.ds(after_two, border), :].astype(jnp.bfloat16)
+            two = grad[plane, block, pl.ds(after_two, border), :].astype(jnp.bfloat16)
+            if block < blocks:
+                out_two[plane, block] = two
+            else:
+                corner_two[plane] = two
     even_col, _ = sides("col", ncols)
     middle = slice(2 * border, rows)
     for pair in range(2):
@@ -350,64 +371,67 @@
         mid_two[pair] = jnp.where(even_col, left, right).astype(jnp.bfloat16)
 
 
-def sides_kernel(ncols, nrows, grad, came_one, came_two, middle, side_one, side_two):
-    blocks = grad.shape[1] - 1
-    border = came_one.shape[2]
+def ends(even_row, inner, one, two):
+    one = one.astype(jnp.float32)
+    two = jnp.where(inner, two.astype(jnp.float32), 0.0)
+    return jnp.where(even_row, two, one), jnp.where(even_row, one, two)
+
+
+def sides_kernel(ncols, nrows, grad, row_one, corner_two, side_one, side_two):
+    blocks = row_one.shape[1] - 1
+    border = row_one.shape[2]
     rows = grad.shape[2] - 2 * border
     even_col, _ = sides("col", ncols)
     even_row, inner = sides("row", nrows)
-
-    def ends(plane, block):
-        one = came_one[plane, block].astype(jnp.float32)
-        two = jnp.where(inner, came_two[plane, block].astype(jnp.float32), 0.0)
-        top = grad[plane, block, border : 2 * border] + jnp.where(even_row, two, one)
-        bottom = grad[plane, block, rows : rows + border] + jnp.where(even_row, one, two)
-        return top, bottom
-
     for pair in range(2):
-        for number, (even, odd) in enumerate(zip(ends(2 * pair, blocks), ends(2 * pair + 1, blocks))):
+        planes = (2 * pair, 2 * pair + 1)
+        came = [ends(even_row, inner, row_one[plane, blocks], corner_two[plane]) for plane in planes]
+        for number, at in enumerate((border, rows)):
+            even, odd = (
+                grad[plane, blocks, at : at + border] + here[number] for plane, here in zip(planes, came)
+            )
             right, left = join_right(even, odd, border), join_left(even, odd, border)
             span = slice(number * border, (number + 1) * border)
             side_one[pair, span] = jnp.where(even_col, right, left).astype(jnp.bfloat16)
             side_two[pair, span] = jnp.where(even_col, left, right).astype(jnp.bfloat16)
-    for plane in range(4):
-        for block in range(blocks):
-            span = slice(block * LANES, (block + 1) * LANES)
-            top, bottom = ends(plane, block)
-            middle[plane, :border, span] = top
-            middle[plane, border : rows - border, span] = grad[plane, block, 2 * border : rows]
-            middle[plane, rows - border :, span] = bottom
-
-
-def final_kernel(ncols, border, middle, mid_one, mid_two, end_one, end_two, out):
-    rows, cols = middle.shape[1:]
+
+
+def final_kernel(ncols, nrows, grad, row_one, row_two, mid_one, mid_two, end_one, end_two, out, whole, sem):
+    blocks, border = row_two.shape[1:3]
+    rows = grad.shape[2] - 2 * border
     low = lax.broadcasted_iota(jnp.int32, (1, LANES), 1) < border
-    even_col, inner = sides("col", ncols)
-    parts = (
-        (slice(0, border), end_one, end_two, slice(0, border)),
-        (slice(border, rows - border), mid_one, mid_two, slice(0, rows - 2 * border)),
-        (slice(rows - border, rows), end_one, end_two, slice(border, 2 * border)),
-    )
-    for span, came_one, came_two, source in parts:
-        for pair in range(2):
-            one = came_one[pair, source].astype(jnp.float32)
-            two = jnp.where(inner, came_two[pair, source].astype(jnp.float32), 0.0)
-            near = jnp.where(even_col, two, one)
-            far = jnp.where(even_col, one, two)
-            even, odd = 2 * pair, 2 * pair + 1
-            for plane, first, last in (
-                (even, near, pltpu.roll(far, border, 1)),
-                (odd, pltpu.roll(near, border, 1), far),
-            ):
-                add_first = jnp.where(low, first, 0.0)
-                add_last = jnp.where(low, 0.0, last)
-                if cols == LANES:
-                    out[plane, span] = middle[plane, span] + add_first + add_last
-                    continue
-                out[plane, span, :LANES] = middle[plane, span, :LANES] + add_first
-                if cols > 2 * LANES:
-                    out[plane, span, LANES : cols - LANES] = middle[plane, span, LANES : cols - LANES]
-                out[plane, span, cols - LANES :] = middle[plane, span, cols - LANES :] + add_last
+    even_col, inner_col = sides("col", ncols)
+    even_row, inner_row = sides("row", nrows)
+    copies = []
+    for pair in range(2):
+        near, far = [], []
+        for came_one, came_two in ((mid_one, mid_two), (end_one, end_two)):
+            one = came_one[pair].astype(jnp.float32)
+            two = jnp.where(inner_col, came_two[pair].astype(jnp.float32), 0.0)
+            near.append(jnp.where(even_col, two, one))
+            far.append(jnp.where(even_col, one, two))
+        near, far = (
+            jnp.concatenate([end[:border], mid, end[border:]], axis=0) for mid, end in (near, far)
+        )
+        for plane, first, last in (
+            (2 * pair, near, pltpu.roll(far, border, 1)),
+            (2 * pair + 1, pltpu.roll(near, border, 1), far),
+        ):
+            for block in range(blocks):
+                span = slice(block * LANES, (block + 1) * LANES)
+                total = grad[plane, block, border : border + rows]
+                if block == 0:
+                    total = total + jnp.where(low, first, 0.0)
+                if block == blocks - 1:
+                    total = total + jnp.where(low, 0.0, last)
+                top, bottom = ends(even_row, inner_row, row_one[plane, block], row_two[plane, block])
+                whole[plane, :border, span] = total[:border] + top
+                whole[plane, border : rows - border, span] = total[border : rows - border]
+                whole[plane, rows - border :, span] = total[rows - border :] + bottom
+            copies.append(pltpu.make_async_copy(whole.at[plane], out.at[plane], sem.at[plane]))
+            copies[-1].start()
+    for copy in copies:
+        copy.wait()
 
 
 def local(ncols, nrows, objects, probe, amplitudes, owners, off_rows, off_cols):
@@ -422,12 +446,12 @@
     bf16 = functools.partial(jax.ShapeDtypeStruct, dtype=jnp.bfloat16)
     f32 = functools.partial(jax.ShapeDtypeStruct, dtype=jnp.float32)
 
-    def kernel(body, ins, outs, name, scratch=(), limit=VMEM_BYTES, cost=None):
+    def kernel(body, ins, outs, name, scratch=(), limit=VMEM_BYTES, cost=None, to=vmem):
         return pl.pallas_call(
             body,
             out_shape=outs,
             in_specs=ins if isinstance(ins, list) else [vmem] * ins,
-            out_specs=[vmem] * len(outs),
+            out_specs=[to] * len(outs),
             scratch_shapes=list(scratch),
             compiler_params=pltpu.CompilerParams(vmem_limit_bytes=limit),
             cost_estimate=cost,
@@ -459,11 +483,15 @@
         "pack",
         [
             pltpu.VMEM(objects.shape, jnp.float32),
+            pltpu.VMEM((2,) + side_shape.shape, jnp.bfloat16),
             pltpu.VMEM((count, width, width), jnp.bfloat16),
+            pltpu.VMEM((kinds, CAP * width + NOTE, LANES), jnp.bfloat16),
             pltpu.SMEM((3,) + owners.shape, jnp.int32),
-            pltpu.SemaphoreType.DMA((5,)),
+            pltpu.SemaphoreType.DMA((10,)),
+            pltpu.SemaphoreType.DMA((kinds,)),
         ],
         FULL_BYTES,
+        to=anywhere,
     )(amplitudes, owners, off_rows, off_cols, objects)
     came_one, came_two = swap(side_one, col_one), swap(side_two, col_two)
     if ncols == 8:
@@ -484,10 +512,12 @@
         obj, side, line_one, line_two
     )
     tables = make_tables(width)
-    grad, line_one, line_two, mid_one, mid_two = kernel(
+    edge_shape = bf16((4, blocks, border, LANES))
+    corner_shape = bf16((4, border, LANES))
+    grad, line_one, edge_two, corner_two, mid_one, mid_two = kernel(
         functools.partial(main_kernel, BATCH, ncols, nrows),
         [anywhere] * 4,
-        [whole] + [line_shape] * 2 + [bf16((2, rows - 2 * border, LANES))] * 2,
+        [whole, line_shape, edge_shape, corner_shape] + [bf16((2, rows - 2 * border, LANES))] * 2,
         "gradients",
         [
             pltpu.VMEM(tables.shape, jnp.bfloat16),
@@ -502,18 +532,21 @@
         MAIN_BYTES,
     )(tables, probe, msgs, ext)
 
-    line_two, line_one = swap(line_two, row_back), swap(line_one, row_one)
+    corner_two, line_one = swap(corner_two, row_back), swap(line_one, row_one)
     mid_one, mid_two = swap(mid_one, col_one), swap(mid_two, col_two)
-    middle, end_one, end_two = kernel(
-        functools.partial(sides_kernel, ncols, nrows),
-        3,
-        [f32((4, rows, cols))] + [bf16((2, 2 * border, LANES))] * 2,
-        "sides",
-    )(grad, line_one, line_two)
+    edge_two = swap(edge_two, row_back)
+    end_one, end_two = kernel(
+        functools.partial(sides_kernel, ncols, nrows), 3, [bf16((2, 2 * border, LANES))] * 2, "sides", cost=pl.CostEstimate(flops=10**10, bytes_accessed=10**6, transcendentals=0)
+    )(grad, line_one, corner_two)
     end_one, end_two = swap(end_one, col_one), swap(end_two, col_two)
     (out,) = kernel(
-        functools.partial(final_kernel, ncols, border), 5, [f32((4, rows, cols))], "final"
-    )(middle, mid_one, mid_two, end_one, end_two)
+        functools.partial(final_kernel, ncols, nrows),
+        7,
+        [f32((4, rows, cols))],
+        "final",
+        [pltpu.VMEM((4, rows, cols), jnp.float32), pltpu.SemaphoreType.DMA((4,))],
+        to=anywhere,
+    )(grad, line_one, edge_two, mid_one, mid_two, end_one, end_two)
     return out.reshape(objects.shape)
 
 

time: 44.4 us -> 43.9 us (0.989)
  starting transfers between devices: 17.5 us -> 15.3 us
  Pallas kernels: 8.91 us -> 11.1 us
    pallas_call x1, Pallas kernels: 4.74 us -> 7.15 us  [local(): kernel(functools.partial(main_kernel, BATCH, ncols, nrows), [anywhere] *...]
    ppermute x10 -> x11, starting transfers between devices: 11.2 us -> 9.01 us  [swap(): return lax.ppermute(array, ('row', 'col'), flat)]
    ppermute x10 -> x11, waiting for transfers between devices: 9.69 us -> 9.5 us  [swap(): return lax.ppermute(array, ('row', 'col'), flat)]
  transfers between devices with their start and end apart: 11 -> 12, of which waited for: 4 -> 5; matrix products, arithmetic and copies ran while one was open for 0% -> 0% of each run, Pallas kernels for 1% -> 1%
where the time goes in v1:
time: 43.9 us; the launch traced here: 43.6 us
  waiting for transfers between devices  15.7 us (36%)
  starting transfers between devices  15.3 us (35%)
  Pallas kernels  11.1 us (25%)
  local copies, waits for them, and re-layouts  1.43 us (3%)
    ppermute x11, waiting for transfers between devices, swap(): return lax.ppermute(array, ('row', 'col'), flat)  9.5 us
    ppermute x11, starting transfers between devices, swap(): return lax.ppermute(array, ('row', 'col'), flat)  9.01 us
    pallas_call x1, Pallas kernels, local(): kernel(functools.partial(main_kernel, BATCH, ncols, nrows), [anywhere] *...  7.15 us
    all_to_all x1, starting transfers between devices, local(): msgs = lax.all_to_all(msgs, 'col', 0, 0)  6.34 us
    all_to_all x1, waiting for transfers between devices, local(): msgs = lax.all_to_all(msgs, 'col', 0, 0)  6.17 us
    pallas_call x1, Pallas kernels, local(): kernel(functools.partial(pack_kernel, ways, ncols), [anywhere] * 5, [side...  2.31 us
    unnamed x8, local copies, waits for them, and re-layouts  1.43 us
    pallas_call x1, Pallas kernels, local(): kernel(functools.partial(final_kernel, ncols, nrows), 7, [f32((4, rows, c...  1.16 us
  transfers between devices with their start and end apart: 12, of which 5 were waited for; matrix products, arithmetic and copies ran while one was open for 0% of the time, Pallas kernels for 1%

profile of v1, /device:TPU:0, one launch (start us, length us, event | category | flops | bytes accessed | tf_op | source)
XLA Modules:
  0.0 43.6 jit_solution(14436775058575636600)
XLA Ops:
  0.0 0.0 copy-start.1
  0.0 2.3 %pack.1 = (bf16[2,256,128]{2,1,0:T(8,128)(2,1)}, bf16[2,256,128]{2,1,0:T(8,128)(2,1)}, bf16[8,272,128]{2,1,0:T(8,128)(2,1)}) custom-call(bf16[1,1,6,128,128]{4,3,2,1,0:T(8,128)(2,1)} %amps.1, s32[1,1,6]{2,1,0:T(1,128)} %owners.1, s32[1,1,6]{2,1,0:T(1,128)} %at_rows.1, s32[1,1,6]{2,1,0:T(1,128)} %at_cols.1, f32[2,2,256,256]{3,2,1,0:T(8,128)} %obj.1), custom_call_target="tpu_custom_call" | custom-call | tf_op jit(solution)/shard_map/pack/pallas_call | solution.py:479
  2.3 3.0 %collective-permute-start = (bf16[2,256,128]{2,1,0:T(8,128)(2,1)}, bf16[2,256,128]{2,1,0:T(8,128)(2,1)S(1)}, u32[]{:S(2)}, u32[]{:S(2)}) collective-permute-start(bf16[2,256,128]{2,1,0:T(8,128)(2,1)} %get-tuple-element.20), channel_id=1, source_target_pairs={{0,1},{1,0},{2,3},{3,2},{4,5},{5,4},{6,7},{7,6},{8,9},{9,8},{10,11... | collective-permute-start | bytes 393224 | tf_op jit(solution)/shard_map/ppermute | solution.py:466
  5.3 0.0 collective-permute-start.1
  5.3 6.3 %all-to-all-start = ((bf16[8,272,128]{2,1,0:T(8,128)(2,1)}), bf16[8,272,128]{2,1,0:T(8,128)(2,1)}, u32[]{:S(2)}, u32[]{:S(2)}) async-start(bf16[8,272,128]{2,1,0:T(8,128)(2,1)} %get-tuple-element.19), calls=%async_computation | async-start | bytes 1114112 | tf_op jit(solution)/shard_map/all_to_all | solution.py:498
  11.7 0.0 collective-permute-done.came_one
  11.7 0.0 collective-permute-done.1.came_two
  11.7 0.0 copy-done.1
  11.7 0.2 rows.1
  11.9 0.0 copy-start.2
  11.9 0.0 copy-start.3
  11.9 0.1 collective-permute-start.2
  12.0 1.6 %collective-permute-start.3 = (bf16[4,3,64,128]{3,2,1,0:T(8,128)(2,1)S(1)}, bf16[4,3,64,128]{3,2,1,0:T(8,128)(2,1)S(1)}, u32[]{:S(2)}, u32[]{:S(2)}) collective-permute-start(bf16[4,3,64,128]{3,2,1,0:T(8,128)(2,1)S(1)} %get-tuple-element.24), channel_id=1, source_target_pairs={{0,24},{1,25},{2,26},{3,27},{4,28},{5,29},{6,30},{7,31},{8,16},{9,... | collective-permute-start | bytes 589832 | tf_op jit(solution)/shard_map/ppermute | solution.py:466
  13.6 0.0 collective-permute-done.2.row_one
  13.6 5.1 %collective-permute-done.3.row_two = bf16[4,3,64,128]{3,2,1,0:T(8,128)(2,1)S(1)} collective-permute-done((bf16[4,3,64,128]{3,2,1,0:T(8,128)(2,1)S(1)}, bf16[4,3,64,128]{3,2,1,0:T(8,128)(2,1)S(1)}, u32[]{:S(2)}, u32[]{:S(2)}) %collective-permute-start.3) | collective-permute-done | bytes 196640 | tf_op jit(solution)/shard_map/ppermute | solution.py:466
  18.7 0.2 extend.1.refs_3_
  18.9 0.0 copy-start
  18.9 1.4 %copy-done = f32[4,3,384,128]{3,2,1,0:T(8,128)} copy-done((f32[4,3,384,128]{3,2,1,0:T(8,128)}, f32[4,3,384,128]{3,2,1,0:T(8,128)S(1)}, u32[]{:S(2)}) %copy-start) | copy-done | bytes 2359320
  20.3 6.2 %all-to-all-done.refs_2_ = bf16[8,272,128]{2,1,0:T(8,128)(2,1)} async-done(((bf16[8,272,128]{2,1,0:T(8,128)(2,1)}), bf16[8,272,128]{2,1,0:T(8,128)(2,1)}, u32[]{:S(2)}, u32[]{:S(2)}) %all-to-all-start) | async-done | bytes 557088 | tf_op jit(solution)/shard_map/all_to_all | solution.py:498
  26.4 0.0 copy-done.2
  26.4 0.0 copy-done.3
  26.4 7.1 %gradients.1 = (f32[4,3,384,128]{3,2,1,0:T(8,128)S(1)}, bf16[4,3,64,128]{3,2,1,0:T(8,128)(2,1)S(1)}, bf16[4,2,64,128]{3,2,1,0:T(8,128)(2,1)S(1)}, bf16[4,64,128]...) custom-call(bf16[4,256,256]{2,1,0:T(8,128)(2,1)S(1)} %copy-done.2, ...), custom_call_target="tpu_custom_call" | custom-call | tf_op jit(solution)/shard_map/gradients/pallas_call | solution.py:517
  33.6 0.1 collective-permute-start.4
  33.7 0.1 collective-permute-start.8
  33.8 0.3 collective-permute-start.6
  34.0 2.6 %collective-permute-start.7 = (bf16[2,128,128]{2,1,0:T(8,128)(2,1)S(1)}, bf16[2,128,128]{2,1,0:T(8,128)(2,1)S(1)}, u32[]{:S(2)}, u32[]{:S(2)}) collective-permute-start(bf16[2,128,128]{2,1,0:T(8,128)(2,1)S(1)} %get-tuple-element.29), channel_id=1, source_target_pairs={{0,8},{8,0},{16,24},{24,16},{1,2},{9,10},{17,18},{25,26},{2,1},{10... | collective-permute-start | bytes 196616 | tf_op jit(solution)/shard_map/ppermute | solution.py:466
  36.6 0.7 %collective-permute-start.5 = (bf16[4,2,64,128]{3,2,1,0:T(8,128)(2,1)S(1)}, bf16[4,2,64,128]{3,2,1,0:T(8,128)(2,1)S(1)}, u32[]{:S(2)}, u32[]{:S(2)}) collective-permute-start(bf16[4,2,64,128]{3,2,1,0:T(8,128)(2,1)S(1)} %get-tuple-element.27), channel_id=1, source_target_pairs={{0,2},{1,3},{2,0},{3,1},{4,6},{5,7},{6,4},{7,5},{8,16},{9,17},{10,... | collective-permute-start | bytes 393224 | tf_op jit(solution)/shard_map/ppermute | solution.py:466
  37.3 0.7 %collective-permute-done.8.corner_two = bf16[4,64,128]{2,1,0:T(8,128)(2,1)S(1)} collective-permute-done((bf16[4,64,128]{2,1,0:T(8,128)(2,1)S(1)}, bf16[4,64,128]{2,1,0:T(8,128)(2,1)S(1)}, u32[]{:S(2)}, u32[]{:S(2)}) %collective-permute-start.8) | collective-permute-done | bytes 65568 | tf_op jit(solution)/shard_map/ppermute | solution.py:466
  38.0 0.0 collective-permute-done.4.row_one
  38.0 0.1 sides.1
  38.1 0.2 collective-permute-start.9
  38.4 0.3 collective-permute-start.10
  38.7 0.0 collective-permute-done.6.mid_one
  38.7 0.0 collective-permute-done.7.mid_two
  38.7 2.9 %collective-permute-done.5.row_two = bf16[4,2,64,128]{3,2,1,0:T(8,128)(2,1)S(1)} collective-permute-done((bf16[4,2,64,128]{3,2,1,0:T(8,128)(2,1)S(1)}, bf16[4,2,64,128]{3,2,1,0:T(8,128)(2,1)S(1)}, u32[]{:S(2)}, u32[]{:S(2)}) %collective-permute-start.5) | collective-permute-done | bytes 131104 | tf_op jit(solution)/shard_map/ppermute | solution.py:466
  41.7 0.8 %collective-permute-done.9.end_one = bf16[2,128,128]{2,1,0:T(8,128)(2,1)S(1)} collective-permute-done((bf16[2,128,128]{2,1,0:T(8,128)(2,1)S(1)}, bf16[2,128,128]{2,1,0:T(8,128)(2,1)S(1)}, u32[]{:S(2)}, u32[]{:S(2)}) %collective-permute-start.9) | collective-permute-done | bytes 65568 | tf_op jit(solution)/shard_map/ppermute | solution.py:466
  42.5 0.0 collective-permute-done.10.end_two
  42.5 1.2 %final.1 = f32[4,256,256]{2,1,0:T(8,128)} custom-call(f32[4,3,384,128]{3,2,1,0:T(8,128)S(1)} %get-tuple-element.25.grad, bf16[4,3,64,128]{3,2,1,0:T(8,128)(2,1)S(1)} %collective-permute-done.4.row_one, bf16[4,2,64,128]{3,2,1,0:T(8,128)(2,1)S(1)} %collective-permute-done.5.row_two, bf16[2,128,128]{2,1,0:T(8,128)(2,1)S(1)} %collective-permute-done.6.mid_one, ...), custom_call_target="tpu_custom_call" | custom-call | tf_op jit(solution)/shard_map/final/pallas_call | solution.py:542
Async XLA Ops:
  0.0 11.7 %copy-start.1 = (f32[2,2,256,256]{3,2,1,0:T(8,128)S(1)}, f32[2,2,256,256]{3,2,1,0:T(8,128)}, u32[]{:S(2)}) copy-start(f32[2,2,256,256]{3,2,1,0:T(8,128)} %obj.1) | copy-start | bytes 3145732
  2.3 9.3 %collective-permute-start = (bf16[2,256,128]{2,1,0:T(8,128)(2,1)}, bf16[2,256,128]{2,1,0:T(8,128)(2,1)S(1)}, u32[]{:S(2)}, u32[]{:S(2)}) collective-permute-start(bf16[2,256,128]{2,1,0:T(8,128)(2,1)} %get-tuple-element.20), channel_id=1, source_target_pairs={{0,1},{1,0},{2,3},{3,2},{4,5},{5,4},{6,7},{7,6},{8,9},{9,8},{10,11... | collective-permute-start | bytes 393224 | tf_op jit(solution)/shard_map/ppermute | solution.py:466
  5.3 6.3 %collective-permute-start.1 = (bf16[2,256,128]{2,1,0:T(8,128)(2,1)}, bf16[2,256,128]{2,1,0:T(8,128)(2,1)S(1)}, u32[]{:S(2)}, u32[]{:S(2)}) collective-permute-start(bf16[2,256,128]{2,1,0:T(8,128)(2,1)} %get-tuple-element.21), channel_id=1, source_target_pairs={{0,8},{8,0},{16,24},{24,16},{1,2},{9,10},{17,18},{25,26},{2,1},{10... | collective-permute-start | bytes 393224 | tf_op jit(solution)/shard_map/ppermute | solution.py:466
  5.3 21.1 %all-to-all-start = ((bf16[8,272,128]{2,1,0:T(8,128)(2,1)}), bf16[8,272,128]{2,1,0:T(8,128)(2,1)}, u32[]{:S(2)}, u32[]{:S(2)}) async-start(bf16[8,272,128]{2,1,0:T(8,128)(2,1)} %get-tuple-element.19), calls=%async_computation | async-start | bytes 1114112 | tf_op jit(solution)/shard_map/all_to_all | solution.py:498
  11.9 14.6 %copy-start.2 = (bf16[4,256,256]{2,1,0:T(8,128)(2,1)S(1)}, bf16[4,256,256]{2,1,0:T(8,128)(2,1)}, u32[]{:S(2)}) copy-start(bf16[4,256,256]{2,1,0:T(8,128)(2,1)} %constant.2.clone.refs_0_) | copy-start | bytes 1572868
  11.9 14.5 %copy-start.3 = (f32[2,2,128,128]{3,2,1,0:T(8,128)S(1)}, f32[2,2,128,128]{3,2,1,0:T(8,128)}, u32[]{:S(2)}) copy-start(f32[2,2,128,128]{3,2,1,0:T(8,128)} %refs_1_.1) | copy-start | bytes 786436
  11.9 1.7 %collective-permute-start.2 = (bf16[4,3,64,128]{3,2,1,0:T(8,128)(2,1)S(1)}, bf16[4,3,64,128]{3,2,1,0:T(8,128)(2,1)S(1)}, u32[]{:S(2)}, u32[]{:S(2)}) collective-permute-start(bf16[4,3,64,128]{3,2,1,0:T(8,128)(2,1)S(1)} %get-tuple-element.23), channel_id=1, source_target_pairs={{0,8},{1,9},{2,10},{3,11},{4,12},{5,13},{6,14},{7,15},{8,0},{9,1},... | collective-permute-start | bytes 589832 | tf_op jit(solution)/shard_map/ppermute | solution.py:466
  12.0 6.7 %collective-permute-start.3 = (bf16[4,3,64,128]{3,2,1,0:T(8,128)(2,1)S(1)}, bf16[4,3,64,128]{3,2,1,0:T(8,128)(2,1)S(1)}, u32[]{:S(2)}, u32[]{:S(2)}) collective-permute-start(bf16[4,3,64,128]{3,2,1,0:T(8,128)(2,1)S(1)} %get-tuple-element.24), channel_id=1, source_target_pairs={{0,24},{1,25},{2,26},{3,27},{4,28},{5,29},{6,30},{7,31},{8,16},{9,... | collective-permute-start | bytes 589832 | tf_op jit(solution)/shard_map/ppermute | solution.py:466
  18.9 1.4 %copy-start = (f32[4,3,384,128]{3,2,1,0:T(8,128)}, f32[4,3,384,128]{3,2,1,0:T(8,128)S(1)}, u32[]{:S(2)}) copy-start(f32[4,3,384,128]{3,2,1,0:T(8,128)S(1)} %extend.1.refs_3_) | copy-start | bytes 7077892
  33.6 4.4 %collective-permute-start.4 = (bf16[4,3,64,128]{3,2,1,0:T(8,128)(2,1)S(1)}, bf16[4,3,64,128]{3,2,1,0:T(8,128)(2,1)S(1)}, u32[]{:S(2)}, u32[]{:S(2)}) collective-permute-start(bf16[4,3,64,128]{3,2,1,0:T(8,128)(2,1)S(1)} %get-tuple-element.26), channel_id=1, source_target_pairs={{0,8},{1,9},{2,10},{3,11},{4,12},{5,13},{6,14},{7,15},{8,0},{9,1},... | collective-permute-start | bytes 589832 | tf_op jit(solution)/shard_map/ppermute | solution.py:466
  33.7 4.3 %collective-permute-start.8 = (bf16[4,64,128]{2,1,0:T(8,128)(2,1)S(1)}, bf16[4,64,128]{2,1,0:T(8,128)(2,1)S(1)}, u32[]{:S(2)}, u32[]{:S(2)}) collective-permute-start(bf16[4,64,128]{2,1,0:T(8,128)(2,1)S(1)} %get-tuple-element.30), channel_id=1, source_target_pairs={{0,2},{1,3},{2,0},{3,1},{4,6},{5,7},{6,4},{7,5},{8,16},{9,17},{10,... | collective-permute-start | bytes 196616 | tf_op jit(solution)/shard_map/ppermute | solution.py:466
  33.8 5.0 %collective-permute-start.6 = (bf16[2,128,128]{2,1,0:T(8,128)(2,1)S(1)}, bf16[2,128,128]{2,1,0:T(8,128)(2,1)S(1)}, u32[]{:S(2)}, u32[]{:S(2)}) collective-permute-start(bf16[2,128,128]{2,1,0:T(8,128)(2,1)S(1)} %get-tuple-element.28), channel_id=1, source_target_pairs={{0,1},{1,0},{2,3},{3,2},{4,5},{5,4},{6,7},{7,6},{8,9},{9,8},{10,11... | collective-permute-start | bytes 196616 | tf_op jit(solution)/shard_map/ppermute | solution.py:466
  34.0 4.7 %collective-permute-start.7 = (bf16[2,128,128]{2,1,0:T(8,128)(2,1)S(1)}, bf16[2,128,128]{2,1,0:T(8,128)(2,1)S(1)}, u32[]{:S(2)}, u32[]{:S(2)}) collective-permute-start(bf16[2,128,128]{2,1,0:T(8,128)(2,1)S(1)} %get-tuple-element.29), channel_id=1, source_target_pairs={{0,8},{8,0},{16,24},{24,16},{1,2},{9,10},{17,18},{25,26},{2,1},{10... | collective-permute-start | bytes 196616 | tf_op jit(solution)/shard_map/ppermute | solution.py:466
  36.6 5.1 %collective-permute-start.5 = (bf16[4,2,64,128]{3,2,1,0:T(8,128)(2,1)S(1)}, bf16[4,2,64,128]{3,2,1,0:T(8,128)(2,1)S(1)}, u32[]{:S(2)}, u32[]{:S(2)}) collective-permute-start(bf16[4,2,64,128]{3,2,1,0:T(8,128)(2,1)S(1)} %get-tuple-element.27), channel_id=1, source_target_pairs={{0,2},{1,3},{2,0},{3,1},{4,6},{5,7},{6,4},{7,5},{8,16},{9,17},{10,... | collective-permute-start | bytes 393224 | tf_op jit(solution)/shard_map/ppermute | solution.py:466
  38.1 4.3 %collective-permute-start.9 = (bf16[2,128,128]{2,1,0:T(8,128)(2,1)S(1)}, bf16[2,128,128]{2,1,0:T(8,128)(2,1)S(1)}, u32[]{:S(2)}, u32[]{:S(2)}) collective-permute-start(bf16[2,128,128]{2,1,0:T(8,128)(2,1)S(1)} %get-tuple-element.31), channel_id=1, source_target_pairs={{0,1},{1,0},{2,3},{3,2},{4,5},{5,4},{6,7},{7,6},{8,9},{9,8},{10,11... | collective-permute-start | bytes 196616 | tf_op jit(solution)/shard_map/ppermute | solution.py:466
  38.4 4.1 %collective-permute-start.10 = (bf16[2,128,128]{2,1,0:T(8,128)(2,1)S(1)}, bf16[2,128,128]{2,1,0:T(8,128)(2,1)S(1)}, u32[]{:S(2)}, u32[]{:S(2)}) collective-permute-start(bf16[2,128,128]{2,1,0:T(8,128)(2,1)S(1)} %get-tuple-element.32), channel_id=1, source_target_pairs={{0,8},{8,0},{16,24},{24,16},{1,2},{9,10},{17,18},{25,26},{2,1},{10... | collective-permute-start | bytes 196616 | tf_op jit(solution)/shard_map/ppermute | solution.py:466

commit v2 on v1

--- a/solution.py
+++ b/solution.py
@@ -396,40 +396,64 @@
             side_two[pair, span] = jnp.where(even_col, left, right).astype(jnp.bfloat16)
 
 
-def final_kernel(ncols, nrows, grad, row_one, row_two, mid_one, mid_two, end_one, end_two, out, whole, sem):
+def column_sums(ncols, border, came_one, came_two, pair):
+    low = lax.broadcasted_iota(jnp.int32, (1, LANES), 1) < border
+    even_col, inner = sides("col", ncols)
+    one = came_one[pair].astype(jnp.float32)
+    two = jnp.where(inner, came_two[pair].astype(jnp.float32), 0.0)
+    near, far = jnp.where(even_col, two, one), jnp.where(even_col, one, two)
+    return (
+        (jnp.where(low, near, 0.0), jnp.where(low, 0.0, pltpu.roll(far, border, 1))),
+        (jnp.where(low, pltpu.roll(near, border, 1), 0.0), jnp.where(low, 0.0, far)),
+    )
+
+
+def middle_kernel(ncols, grad, mid_one, mid_two, out, whole, sem):
+    height, cols = whole.shape[1:]
+    border = (out.shape[1] - height) // 2
+    blocks = cols // LANES
+    copies = []
+    for pair in range(2):
+        for odd, (first, last) in enumerate(column_sums(ncols, border, mid_one, mid_two, pair)):
+            plane = 2 * pair + odd
+            for block in range(blocks):
+                total = grad[plane, block, 2 * border : 2 * border + height]
+                if block == 0:
+                    total = total + first
+                if block == blocks - 1:
+                    total = total + last
+                whole[plane, :, block * LANES : (block + 1) * LANES] = total
+            span = pl.ds(border, height)
+            copies.append(pltpu.make_async_copy(whole.at[plane], out.at[plane, span], sem.at[plane]))
+            copies[-1].start()
+    for copy in copies:
+        copy.wait()
+
+
+def final_kernel(ncols, nrows, grad, row_one, row_two, end_one, end_two, begun, out, whole, sem):
     blocks, border = row_two.shape[1:3]
     rows = grad.shape[2] - 2 * border
-    low = lax.broadcasted_iota(jnp.int32, (1, LANES), 1) < border
-    even_col, inner_col = sides("col", ncols)
-    even_row, inner_row = sides("row", nrows)
+    even_row, inner = sides("row", nrows)
     copies = []
     for pair in range(2):
-        near, far = [], []
-        for came_one, came_two in ((mid_one, mid_two), (end_one, end_two)):
-            one = came_one[pair].astype(jnp.float32)
-            two = jnp.where(inner_col, came_two[pair].astype(jnp.float32), 0.0)
-            near.append(jnp.where(even_col, two, one))
-            far.append(jnp.where(even_col, one, two))
-        near, far = (
-            jnp.concatenate([end[:border], mid, end[border:]], axis=0) for mid, end in (near, far)
-        )
-        for plane, first, last in (
-            (2 * pair, near, pltpu.roll(far, border, 1)),
-            (2 * pair + 1, pltpu.roll(near, border, 1), far),
-        ):
+        for odd, (first, last) in enumerate(column_sums(ncols, border, end_one, end_two, pair)):
+            plane = 2 * pair + odd
             for block in range(blocks):
-                span = slice(block * LANES, (block + 1) * LANES)
-                total = grad[plane, block, border : border + rows]
-                if block == 0:
-                    total = total + jnp.where(low, first, 0.0)
-                if block == blocks - 1:
-                    total = total + jnp.where(low, 0.0, last)
-                top, bottom = ends(even_row, inner_row, row_one[plane, block], row_two[plane, block])
-                whole[plane, :border, span] = total[:border] + top
-                whole[plane, border : rows - border, span] = total[border : rows - border]
-                whole[plane, rows - border :, span] = total[rows - border :] + bottom
-            copies.append(pltpu.make_async_copy(whole.at[plane], out.at[plane], sem.at[plane]))
-            copies[-1].start()
+                came = ends(even_row, inner, row_one[plane, block], row_two[plane, block])
+                for number, at in enumerate((border, rows)):
+                    span = slice(number * border, (number + 1) * border)
+                    total = grad[plane, block, at : at + border] + came[number]
+                    if block == 0:
+                        total = total + first[span]
+                    if block == blocks - 1:
+                        total = total + last[span]
+                    whole[plane, span, block * LANES : (block + 1) * LANES] = total
+            for number, at in enumerate((0, rows - border)):
+                source = whole.at[plane, pl.ds(number * border, border)]
+                copies.append(
+                    pltpu.make_async_copy(source, out.at[plane, pl.ds(at, border)], sem.at[plane, number])
+                )
+                copies[-1].start()
     for copy in copies:
         copy.wait()
 
@@ -446,7 +470,7 @@
     bf16 = functools.partial(jax.ShapeDtypeStruct, dtype=jnp.bfloat16)
     f32 = functools.partial(jax.ShapeDtypeStruct, dtype=jnp.float32)
 
-    def kernel(body, ins, outs, name, scratch=(), limit=VMEM_BYTES, cost=None, to=vmem):
+    def kernel(body, ins, outs, name, scratch=(), limit=VMEM_BYTES, cost=None, to=vmem, alias={}):
         return pl.pallas_call(
             body,
             out_shape=outs,
@@ -455,6 +479,7 @@
             scratch_shapes=list(scratch),
             compiler_params=pltpu.CompilerParams(vmem_limit_bytes=limit),
             cost_estimate=cost,
+            input_output_aliases=alias,
             name=name,
         )
 
@@ -466,7 +491,6 @@
         return lax.ppermute(array, ("row", "col"), flat)
 
     row_one, row_two = row_partners(nrows, ncols, lambda r, c: (nrows - 1 - r, c))
-    _, row_back = row_partners(nrows, ncols, lambda r, c: (r, c ^ 2))
     col_one, col_two = col_partners(nrows, ncols)
     if ncols == 8:
         ways = [functools.partial(lambda to, at: to, to) for to in range(ncols)]
@@ -532,21 +556,31 @@
         MAIN_BYTES,
     )(tables, probe, msgs, ext)
 
-    corner_two, line_one = swap(corner_two, row_back), swap(line_one, row_one)
+    corner_two, line_one = swap(corner_two, row_two), swap(line_one, row_one)
     mid_one, mid_two = swap(mid_one, col_one), swap(mid_two, col_two)
-    edge_two = swap(edge_two, row_back)
+    edge_two = swap(edge_two, row_two)
     end_one, end_two = kernel(
         functools.partial(sides_kernel, ncols, nrows), 3, [bf16((2, 2 * border, LANES))] * 2, "sides", cost=pl.CostEstimate(flops=10**10, bytes_accessed=10**6, transcendentals=0)
     )(grad, line_one, corner_two)
     end_one, end_two = swap(end_one, col_one), swap(end_two, col_two)
+    whole_shape = f32((4, rows, cols))
+    (out,) = kernel(
+        functools.partial(middle_kernel, ncols),
+        3,
+        [whole_shape],
+        "middle",
+        [pltpu.VMEM((4, rows - 2 * border, cols), jnp.float32), pltpu.SemaphoreType.DMA((4,))],
+        to=anywhere,
+    )(grad, mid_one, mid_two)
     (out,) = kernel(
         functools.partial(final_kernel, ncols, nrows),
-        7,
-        [f32((4, rows, cols))],
+        [vmem] * 5 + [anywhere],
+        [whole_shape],
         "final",
-        [pltpu.VMEM((4, rows, cols), jnp.float32), pltpu.SemaphoreType.DMA((4,))],
+        [pltpu.VMEM((4, 2 * border, cols), jnp.float32), pltpu.SemaphoreType.DMA((4, 2))],
         to=anywhere,
-    )(grad, line_one, edge_two, mid_one, mid_two, end_one, end_two)
+        alias={5: 0},
+    )(grad, line_one, edge_two, end_one, end_two, out)
     return out.reshape(objects.shape)
 
 

time: 43.9 us -> 43.7 us (level)
  the two profiles are of different devices: /device:TPU:0 before, /device:TPU:13 now
where the time goes in v2:
time: 43.7 us; the launch traced here: 42.9 us
  starting transfers between devices  15 us (34%)
  waiting for transfers between devices  14.5 us (33%)
  Pallas kernels  11.8 us (27%)
  local copies, waits for them, and re-layouts  1.43 us (3%)
    ppermute x11, waiting for transfers between devices, swap(): return lax.ppermute(array, ('row', 'col'), flat)  13.6 us
    ppermute x11, starting transfers between devices, swap(): return lax.ppermute(array, ('row', 'col'), flat)  9.24 us
    pallas_call x1, Pallas kernels, local(): kernel(functools.partial(main_kernel, BATCH, ncols, nrows), [anywhere] *...  7.19 us
    all_to_all x1, starting transfers between devices, local(): msgs = lax.all_to_all(msgs, 'col', 0, 0)  5.81 us
    pallas_call x1, Pallas kernels, local(): kernel(functools.partial(pack_kernel, ways, ncols), [anywhere] * 5, [side...  2.31 us
    unnamed x8, local copies, waits for them, and re-layouts  1.43 us
    pallas_call x1, Pallas kernels, local(): kernel(functools.partial(final_kernel, ncols, nrows), [vmem] * 5 + [anywh...  0.96 us
    pallas_call x1, Pallas kernels, local(): kernel(functools.partial(middle_kernel, ncols), 3, [whole_shape], 'middle...  0.91 us
  transfers between devices with their start and end apart: 12, of which 6 were waited for; matrix products, arithmetic and copies ran while one was open for 0% of the time, Pallas kernels for 3%

profile of v2, /device:TPU:13, one launch (start us, length us, event | category | flops | bytes accessed | tf_op | source)
XLA Modules:
  0.0 42.9 jit_solution(16730879556331625266)
XLA Ops:
  0.0 0.0 copy-start.1
  0.0 2.3 %pack.1 = (bf16[2,256,128]{2,1,0:T(8,128)(2,1)}, bf16[2,256,128]{2,1,0:T(8,128)(2,1)}, bf16[8,272,128]{2,1,0:T(8,128)(2,1)}) custom-call(bf16[1,1,6,128,128]{4,3,2,1,0:T(8,128)(2,1)} %amps.1, s32[1,1,6]{2,1,0:T(1,128)} %owners.1, s32[1,1,6]{2,1,0:T(1,128)} %at_rows.1, s32[1,1,6]{2,1,0:T(1,128)} %at_cols.1, f32[2,2,256,256]{3,2,1,0:T(8,128)} %obj.1), custom_call_target="tpu_custom_call" | custom-call | tf_op jit(solution)/shard_map/pack/pallas_call | solution.py:503
  2.3 1.3 %collective-permute-start = (bf16[2,256,128]{2,1,0:T(8,128)(2,1)}, bf16[2,256,128]{2,1,0:T(8,128)(2,1)S(1)}, u32[]{:S(2)}, u32[]{:S(2)}) collective-permute-start(bf16[2,256,128]{2,1,0:T(8,128)(2,1)} %get-tuple-element.20), channel_id=1, source_target_pairs={{0,1},{1,0},{2,3},{3,2},{4,5},{5,4},{6,7},{7,6},{8,9},{9,8},{10,11... | collective-permute-start | bytes 393224 | tf_op jit(solution)/shard_map/ppermute | solution.py:491
  3.6 0.1 collective-permute-start.1
  3.7 5.8 %all-to-all-start = ((bf16[8,272,128]{2,1,0:T(8,128)(2,1)}), bf16[8,272,128]{2,1,0:T(8,128)(2,1)}, u32[]{:S(2)}, u32[]{:S(2)}) async-start(bf16[8,272,128]{2,1,0:T(8,128)(2,1)} %get-tuple-element.19), calls=%async_computation | async-start | bytes 1114112 | tf_op jit(solution)/shard_map/all_to_all | solution.py:522
  9.5 0.0 collective-permute-done.came_one
  9.5 0.0 collective-permute-done.1.came_two
  9.6 0.0 copy-done.1
  9.6 0.2 rows.1
  9.8 0.0 copy-start.2
  9.8 0.0 copy-start.3
  9.8 1.9 %collective-permute-start.2 = (bf16[4,3,64,128]{3,2,1,0:T(8,128)(2,1)S(1)}, bf16[4,3,64,128]{3,2,1,0:T(8,128)(2,1)S(1)}, u32[]{:S(2)}, u32[]{:S(2)}) collective-permute-start(bf16[4,3,64,128]{3,2,1,0:T(8,128)(2,1)S(1)} %get-tuple-element.23), channel_id=1, source_target_pairs={{0,8},{1,9},{2,10},{3,11},{4,12},{5,13},{6,14},{7,15},{8,0},{9,1},... | collective-permute-start | bytes 589832 | tf_op jit(solution)/shard_map/ppermute | solution.py:491
  11.6 0.2 collective-permute-start.3
  11.8 0.9 %collective-permute-done.2.row_one = bf16[4,3,64,128]{3,2,1,0:T(8,128)(2,1)S(1)} collective-permute-done((bf16[4,3,64,128]{3,2,1,0:T(8,128)(2,1)S(1)}, bf16[4,3,64,128]{3,2,1,0:T(8,128)(2,1)S(1)}, u32[]{:S(2)}, u32[]{:S(2)}) %collective-permute-start.2) | collective-permute-done | bytes 196640 | tf_op jit(solution)/shard_map/ppermute | solution.py:491
  12.7 5.9 %collective-permute-done.3.row_two = bf16[4,3,64,128]{3,2,1,0:T(8,128)(2,1)S(1)} collective-permute-done((bf16[4,3,64,128]{3,2,1,0:T(8,128)(2,1)S(1)}, bf16[4,3,64,128]{3,2,1,0:T(8,128)(2,1)S(1)}, u32[]{:S(2)}, u32[]{:S(2)}) %collective-permute-start.3) | collective-permute-done | bytes 196640 | tf_op jit(solution)/shard_map/ppermute | solution.py:491
  18.6 0.2 extend.1.refs_3_
  18.8 0.0 copy-start
  18.8 1.4 %copy-done = f32[4,3,384,128]{3,2,1,0:T(8,128)} copy-done((f32[4,3,384,128]{3,2,1,0:T(8,128)}, f32[4,3,384,128]{3,2,1,0:T(8,128)S(1)}, u32[]{:S(2)}) %copy-start) | copy-done | bytes 2359320
  20.2 0.9 %all-to-all-done.refs_2_ = bf16[8,272,128]{2,1,0:T(8,128)(2,1)} async-done(((bf16[8,272,128]{2,1,0:T(8,128)(2,1)}), bf16[8,272,128]{2,1,0:T(8,128)(2,1)}, u32[]{:S(2)}, u32[]{:S(2)}) %all-to-all-start) | async-done | bytes 557088 | tf_op jit(solution)/shard_map/all_to_all | solution.py:522
  21.1 0.0 copy-done.2
  21.1 0.0 copy-done.3
  21.1 7.2 %gradients.1 = (f32[4,3,384,128]{3,2,1,0:T(8,128)S(1)}, bf16[4,3,64,128]{3,2,1,0:T(8,128)(2,1)S(1)}, bf16[4,2,64,128]{3,2,1,0:T(8,128)(2,1)S(1)}, bf16[4,64,128]...) custom-call(bf16[4,256,256]{2,1,0:T(8,128)(2,1)S(1)} %copy-done.2, ...), custom_call_target="tpu_custom_call" | custom-call | tf_op jit(solution)/shard_map/gradients/pallas_call | solution.py:541
  28.3 3.6 %collective-permute-start.4 = (bf16[4,3,64,128]{3,2,1,0:T(8,128)(2,1)S(1)}, bf16[4,3,64,128]{3,2,1,0:T(8,128)(2,1)S(1)}, u32[]{:S(2)}, u32[]{:S(2)}) collective-permute-start(bf16[4,3,64,128]{3,2,1,0:T(8,128)(2,1)S(1)} %get-tuple-element.26), channel_id=1, source_target_pairs={{0,8},{1,9},{2,10},{3,11},{4,12},{5,13},{6,14},{7,15},{8,0},{9,1},... | collective-permute-start | bytes 589832 | tf_op jit(solution)/shard_map/ppermute | solution.py:491
  31.9 0.0 collective-permute-start.6
  31.9 0.0 collective-permute-start.9
  31.9 0.6 %collective-permute-start.10 = (bf16[2,128,128]{2,1,0:T(8,128)(2,1)S(1)}, bf16[2,128,128]{2,1,0:T(8,128)(2,1)S(1)}, u32[]{:S(2)}, u32[]{:S(2)}) collective-permute-start(bf16[2,128,128]{2,1,0:T(8,128)(2,1)S(1)} %get-tuple-element.32), channel_id=1, source_target_pairs={{0,8},{8,0},{16,24},{24,16},{1,2},{9,10},{17,18},{25,26},{2,1},{10... | collective-permute-start | bytes 196616 | tf_op jit(solution)/shard_map/ppermute | solution.py:491
  32.5 1.4 %collective-permute-start.5 = (bf16[4,2,64,128]{3,2,1,0:T(8,128)(2,1)S(1)}, bf16[4,2,64,128]{3,2,1,0:T(8,128)(2,1)S(1)}, u32[]{:S(2)}, u32[]{:S(2)}) collective-permute-start(bf16[4,2,64,128]{3,2,1,0:T(8,128)(2,1)S(1)} %get-tuple-element.27), channel_id=1, source_target_pairs={{0,24},{1,25},{2,26},{3,27},{4,28},{5,29},{6,30},{7,31},{8,16},{9,... | collective-permute-start | bytes 393224 | tf_op jit(solution)/shard_map/ppermute | solution.py:491
  33.9 2.4 %collective-permute-done.6.corner_two = bf16[4,64,128]{2,1,0:T(8,128)(2,1)S(1)} collective-permute-done((bf16[4,64,128]{2,1,0:T(8,128)(2,1)S(1)}, bf16[4,64,128]{2,1,0:T(8,128)(2,1)S(1)}, u32[]{:S(2)}, u32[]{:S(2)}) %collective-permute-start.6) | collective-permute-done | bytes 65568 | tf_op jit(solution)/shard_map/ppermute | solution.py:491
  36.3 0.0 collective-permute-done.4.row_one
  36.3 0.1 sides.1
  36.5 0.1 collective-permute-start.7
  36.5 0.1 collective-permute-start.8
  36.6 0.0 collective-permute-done.9.mid_one
  36.6 0.0 collective-permute-done.10.mid_two
  36.6 0.9 %middle.1.begun = f32[4,256,256]{2,1,0:T(8,128)} custom-call(f32[4,3,384,128]{3,2,1,0:T(8,128)S(1)} %get-tuple-element.25.grad, bf16[2,128,128]{2,1,0:T(8,128)(2,1)S(1)} %collective-permute-done.9.mid_one, bf16[2,128,128]{2,1,0:T(8,128)(2,1)S(1)} %collective-permute-done.10.mid_two), custom_call_target="tpu_custom_call" | custom-call | tf_op jit(solution)/shard_map/middle/pallas_call | solution.py:567
  37.6 1.0 %collective-permute-done.5.row_two = bf16[4,2,64,128]{3,2,1,0:T(8,128)(2,1)S(1)} collective-permute-done((bf16[4,2,64,128]{3,2,1,0:T(8,128)(2,1)S(1)}, bf16[4,2,64,128]{3,2,1,0:T(8,128)(2,1)S(1)}, u32[]{:S(2)}, u32[]{:S(2)}) %collective-permute-start.5) | collective-permute-done | bytes 131104 | tf_op jit(solution)/shard_map/ppermute | solution.py:491
  38.5 3.4 %collective-permute-done.7.end_one = bf16[2,128,128]{2,1,0:T(8,128)(2,1)S(1)} collective-permute-done((bf16[2,128,128]{2,1,0:T(8,128)(2,1)S(1)}, bf16[2,128,128]{2,1,0:T(8,128)(2,1)S(1)}, u32[]{:S(2)}, u32[]{:S(2)}) %collective-permute-start.7) | collective-permute-done | bytes 65568 | tf_op jit(solution)/shard_map/ppermute | solution.py:491
  42.0 0.0 collective-permute-done.8.end_two
  42.0 1.0 %final.1 = f32[4,256,256]{2,1,0:T(8,128)} custom-call(f32[4,3,384,128]{3,2,1,0:T(8,128)S(1)} %get-tuple-element.25.grad, bf16[4,3,64,128]{3,2,1,0:T(8,128)(2,1)S(1)} %collective-permute-done.4.row_one, bf16[4,2,64,128]{3,2,1,0:T(8,128)(2,1)S(1)} %collective-permute-done.5.row_two, ...), custom_call_target="tpu_custom_call", output_to_operand_aliasing={{}: (5, {})} | custom-call | tf_op jit(solution)/shard_map/final/pallas_call | solution.py:575
Async XLA Ops:
  0.0 9.6 %copy-start.1 = (f32[2,2,256,256]{3,2,1,0:T(8,128)S(1)}, f32[2,2,256,256]{3,2,1,0:T(8,128)}, u32[]{:S(2)}) copy-start(f32[2,2,256,256]{3,2,1,0:T(8,128)} %obj.1) | copy-start | bytes 3145732
  2.3 7.2 %collective-permute-start = (bf16[2,256,128]{2,1,0:T(8,128)(2,1)}, bf16[2,256,128]{2,1,0:T(8,128)(2,1)S(1)}, u32[]{:S(2)}, u32[]{:S(2)}) collective-permute-start(bf16[2,256,128]{2,1,0:T(8,128)(2,1)} %get-tuple-element.20), channel_id=1, source_target_pairs={{0,1},{1,0},{2,3},{3,2},{4,5},{5,4},{6,7},{7,6},{8,9},{9,8},{10,11... | collective-permute-start | bytes 393224 | tf_op jit(solution)/shard_map/ppermute | solution.py:491
  3.6 6.0 %collective-permute-start.1 = (bf16[2,256,128]{2,1,0:T(8,128)(2,1)}, bf16[2,256,128]{2,1,0:T(8,128)(2,1)S(1)}, u32[]{:S(2)}, u32[]{:S(2)}) collective-permute-start(bf16[2,256,128]{2,1,0:T(8,128)(2,1)} %get-tuple-element.21), channel_id=1, source_target_pairs={{0,8},{8,0},{16,24},{24,16},{1,2},{9,10},{17,18},{25,26},{2,1},{10... | collective-permute-start | bytes 393224 | tf_op jit(solution)/shard_map/ppermute | solution.py:491
  3.7 17.4 %all-to-all-start = ((bf16[8,272,128]{2,1,0:T(8,128)(2,1)}), bf16[8,272,128]{2,1,0:T(8,128)(2,1)}, u32[]{:S(2)}, u32[]{:S(2)}) async-start(bf16[8,272,128]{2,1,0:T(8,128)(2,1)} %get-tuple-element.19), calls=%async_computation | async-start | bytes 1114112 | tf_op jit(solution)/shard_map/all_to_all | solution.py:522
  9.8 11.4 %copy-start.2 = (bf16[4,256,256]{2,1,0:T(8,128)(2,1)S(1)}, bf16[4,256,256]{2,1,0:T(8,128)(2,1)}, u32[]{:S(2)}) copy-start(bf16[4,256,256]{2,1,0:T(8,128)(2,1)} %constant.2.clone.refs_0_) | copy-start | bytes 1572868
  9.8 11.3 %copy-start.3 = (f32[2,2,128,128]{3,2,1,0:T(8,128)S(1)}, f32[2,2,128,128]{3,2,1,0:T(8,128)}, u32[]{:S(2)}) copy-start(f32[2,2,128,128]{3,2,1,0:T(8,128)} %refs_1_.1) | copy-start | bytes 786436
  9.8 2.9 %collective-permute-start.2 = (bf16[4,3,64,128]{3,2,1,0:T(8,128)(2,1)S(1)}, bf16[4,3,64,128]{3,2,1,0:T(8,128)(2,1)S(1)}, u32[]{:S(2)}, u32[]{:S(2)}) collective-permute-start(bf16[4,3,64,128]{3,2,1,0:T(8,128)(2,1)S(1)} %get-tuple-element.23), channel_id=1, source_target_pairs={{0,8},{1,9},{2,10},{3,11},{4,12},{5,13},{6,14},{7,15},{8,0},{9,1},... | collective-permute-start | bytes 589832 | tf_op jit(solution)/shard_map/ppermute | solution.py:491
  11.6 7.0 %collective-permute-start.3 = (bf16[4,3,64,128]{3,2,1,0:T(8,128)(2,1)S(1)}, bf16[4,3,64,128]{3,2,1,0:T(8,128)(2,1)S(1)}, u32[]{:S(2)}, u32[]{:S(2)}) collective-permute-start(bf16[4,3,64,128]{3,2,1,0:T(8,128)(2,1)S(1)} %get-tuple-element.24), channel_id=1, source_target_pairs={{0,24},{1,25},{2,26},{3,27},{4,28},{5,29},{6,30},{7,31},{8,16},{9,... | collective-permute-start | bytes 589832 | tf_op jit(solution)/shard_map/ppermute | solution.py:491
  18.8 1.4 %copy-start = (f32[4,3,384,128]{3,2,1,0:T(8,128)}, f32[4,3,384,128]{3,2,1,0:T(8,128)S(1)}, u32[]{:S(2)}) copy-start(f32[4,3,384,128]{3,2,1,0:T(8,128)S(1)} %extend.1.refs_3_) | copy-start | bytes 7077892
  28.3 8.0 %collective-permute-start.4 = (bf16[4,3,64,128]{3,2,1,0:T(8,128)(2,1)S(1)}, bf16[4,3,64,128]{3,2,1,0:T(8,128)(2,1)S(1)}, u32[]{:S(2)}, u32[]{:S(2)}) collective-permute-start(bf16[4,3,64,128]{3,2,1,0:T(8,128)(2,1)S(1)} %get-tuple-element.26), channel_id=1, source_target_pairs={{0,8},{1,9},{2,10},{3,11},{4,12},{5,13},{6,14},{7,15},{8,0},{9,1},... | collective-permute-start | bytes 589832 | tf_op jit(solution)/shard_map/ppermute | solution.py:491
  31.9 4.4 %collective-permute-start.6 = (bf16[4,64,128]{2,1,0:T(8,128)(2,1)S(1)}, bf16[4,64,128]{2,1,0:T(8,128)(2,1)S(1)}, u32[]{:S(2)}, u32[]{:S(2)}) collective-permute-start(bf16[4,64,128]{2,1,0:T(8,128)(2,1)S(1)} %get-tuple-element.28), channel_id=1, source_target_pairs={{0,24},{1,25},{2,26},{3,27},{4,28},{5,29},{6,30},{7,31},{8,16},{9,... | collective-permute-start | bytes 196616 | tf_op jit(solution)/shard_map/ppermute | solution.py:491
  31.9 4.7 %collective-permute-start.9 = (bf16[2,128,128]{2,1,0:T(8,128)(2,1)S(1)}, bf16[2,128,128]{2,1,0:T(8,128)(2,1)S(1)}, u32[]{:S(2)}, u32[]{:S(2)}) collective-permute-start(bf16[2,128,128]{2,1,0:T(8,128)(2,1)S(1)} %get-tuple-element.31), channel_id=1, source_target_pairs={{0,1},{1,0},{2,3},{3,2},{4,5},{5,4},{6,7},{7,6},{8,9},{9,8},{10,11... | collective-permute-start | bytes 196616 | tf_op jit(solution)/shard_map/ppermute | solution.py:491
  31.9 4.7 %collective-permute-start.10 = (bf16[2,128,128]{2,1,0:T(8,128)(2,1)S(1)}, bf16[2,128,128]{2,1,0:T(8,128)(2,1)S(1)}, u32[]{:S(2)}, u32[]{:S(2)}) collective-permute-start(bf16[2,128,128]{2,1,0:T(8,128)(2,1)S(1)} %get-tuple-element.32), channel_id=1, source_target_pairs={{0,8},{8,0},{16,24},{24,16},{1,2},{9,10},{17,18},{25,26},{2,1},{10... | collective-permute-start | bytes 196616 | tf_op jit(solution)/shard_map/ppermute | solution.py:491
  32.5 6.0 %collective-permute-start.5 = (bf16[4,2,64,128]{3,2,1,0:T(8,128)(2,1)S(1)}, bf16[4,2,64,128]{3,2,1,0:T(8,128)(2,1)S(1)}, u32[]{:S(2)}, u32[]{:S(2)}) collective-permute-start(bf16[4,2,64,128]{3,2,1,0:T(8,128)(2,1)S(1)} %get-tuple-element.27), channel_id=1, source_target_pairs={{0,24},{1,25},{2,26},{3,27},{4,28},{5,29},{6,30},{7,31},{8,16},{9,... | collective-permute-start | bytes 393224 | tf_op jit(solution)/shard_map/ppermute | solution.py:491
  36.5 5.5 %collective-permute-start.7 = (bf16[2,128,128]{2,1,0:T(8,128)(2,1)S(1)}, bf16[2,128,128]{2,1,0:T(8,128)(2,1)S(1)}, u32[]{:S(2)}, u32[]{:S(2)}) collective-permute-start(bf16[2,128,128]{2,1,0:T(8,128)(2,1)S(1)} %get-tuple-element.29), channel_id=1, source_target_pairs={{0,1},{1,0},{2,3},{3,2},{4,5},{5,4},{6,7},{7,6},{8,9},{9,8},{10,11... | collective-permute-start | bytes 196616 | tf_op jit(solution)/shard_map/ppermute | solution.py:491
  36.5 5.4 %collective-permute-start.8 = (bf16[2,128,128]{2,1,0:T(8,128)(2,1)S(1)}, bf16[2,128,128]{2,1,0:T(8,128)(2,1)S(1)}, u32[]{:S(2)}, u32[]{:S(2)}) collective-permute-start(bf16[2,128,128]{2,1,0:T(8,128)(2,1)S(1)} %get-tuple-element.30), channel_id=1, source_target_pairs={{0,8},{8,0},{16,24},{24,16},{1,2},{9,10},{17,18},{25,26},{2,1},{10... | collective-permute-start | bytes 196616 | tf_op jit(solution)/shard_map/ppermute | solution.py:491

commit v3 on v2

--- a/solution.py
+++ b/solution.py
@@ -220,9 +220,9 @@
             )
 
 
-def main_kernel(batch, ncols, nrows, *refs):
+def main_kernel(batch, nrows, *refs):
     (given_tables, given_probe, given_msgs, given_ext), refs = refs[:4], refs[4:]
-    (grad, out_one, out_two, corner_two, mid_one, mid_two), refs = refs[:6], refs[6:]
+    (grad, out_one, out_two, corner_two), refs = refs[:4], refs[4:]
     tables, probe, msgs, ext, notes, notes_s, order, sem = refs
     kinds = msgs.shape[0]
     width = probe.shape[2]
@@ -362,38 +362,55 @@
                 out_two[plane, block] = two
             else:
                 corner_two[plane] = two
+
+
+def pack_sides(ncols, even, odd, border):
     even_col, _ = sides("col", ncols)
-    middle = slice(2 * border, rows)
-    for pair in range(2):
-        even, odd = grad[2 * pair, blocks, middle], grad[2 * pair + 1, blocks, middle]
-        right, left = join_right(even, odd, border), join_left(even, odd, border)
-        mid_one[pair] = jnp.where(even_col, right, left).astype(jnp.bfloat16)
-        mid_two[pair] = jnp.where(even_col, left, right).astype(jnp.bfloat16)
-
-
-def ends(even_row, inner, one, two):
-    one = one.astype(jnp.float32)
-    two = jnp.where(inner, two.astype(jnp.float32), 0.0)
-    return jnp.where(even_row, two, one), jnp.where(even_row, one, two)
-
-
-def sides_kernel(ncols, nrows, grad, row_one, corner_two, side_one, side_two):
+    right, left = join_right(even, odd, border), join_left(even, odd, border)
+    return jnp.where(even_col, right, left).astype(jnp.bfloat16), jnp.where(even_col, left, right).astype(jnp.bfloat16)
+
+
+def row_parts(nrows, rows, border):
+    even_row, inner = sides("row", nrows)
+    most = pl.multiple_of(jnp.where(even_row, border, 0), border)
+    rest = pl.multiple_of(jnp.where(even_row, 0, rows - border), border)
+    return even_row, inner, most, rest
+
+
+def with_rows(even_row, region, came):
+    border = came.shape[0]
+    came = came.astype(jnp.float32)
+    top = region[:border] + jnp.where(even_row, 0.0, came)
+    bottom = region[-border:] + jnp.where(even_row, came, 0.0)
+    return jnp.concatenate([top, region[border:-border], bottom], axis=0)
+
+
+def most_kernel(ncols, nrows, grad, row_one, side_one, side_two):
     blocks = row_one.shape[1] - 1
     border = row_one.shape[2]
     rows = grad.shape[2] - 2 * border
-    even_col, _ = sides("col", ncols)
-    even_row, inner = sides("row", nrows)
+    height = rows - border
+    even_row, _, most, _ = row_parts(nrows, rows, border)
     for pair in range(2):
-        planes = (2 * pair, 2 * pair + 1)
-        came = [ends(even_row, inner, row_one[plane, blocks], corner_two[plane]) for plane in planes]
-        for number, at in enumerate((border, rows)):
-            even, odd = (
-                grad[plane, blocks, at : at + border] + here[number] for plane, here in zip(planes, came)
-            )
-            right, left = join_right(even, odd, border), join_left(even, odd, border)
-            span = slice(number * border, (number + 1) * border)
-            side_one[pair, span] = jnp.where(even_col, right, left).astype(jnp.bfloat16)
-            side_two[pair, span] = jnp.where(even_col, left, right).astype(jnp.bfloat16)
+        even, odd = (
+            with_rows(even_row, grad[plane, blocks, pl.ds(border + most, height), :], row_one[plane, blocks])
+            for plane in (2 * pair, 2 * pair + 1)
+        )
+        side_one[pair], side_two[pair] = pack_sides(ncols, even, odd, border)
+
+
+def sides_kernel(ncols, nrows, grad, corner_two, side_one, side_two):
+    blocks = grad.shape[1] - 1
+    border = corner_two.shape[1]
+    rows = grad.shape[2] - 2 * border
+    _, inner, _, rest = row_parts(nrows, rows, border)
+    for pair in range(2):
+        even, odd = (
+            grad[plane, blocks, pl.ds(border + rest, border), :]
+            + jnp.where(inner, corner_two[plane].astype(jnp.float32), 0.0)
+            for plane in (2 * pair, 2 * pair + 1)
+        )
+        side_one[pair], side_two[pair] = pack_sides(ncols, even, odd, border)
 
 
 def column_sums(ncols, border, came_one, came_two, pair):
@@ -408,52 +425,57 @@
     )
 
 
-def middle_kernel(ncols, grad, mid_one, mid_two, out, whole, sem):
+def middle_kernel(ncols, nrows, grad, row_one, mid_one, mid_two, out, whole, sem):
     height, cols = whole.shape[1:]
-    border = (out.shape[1] - height) // 2
+    rows = out.shape[1]
+    border = rows - height
     blocks = cols // LANES
+    even_row, _, most, _ = row_parts(nrows, rows, border)
     copies = []
     for pair in range(2):
         for odd, (first, last) in enumerate(column_sums(ncols, border, mid_one, mid_two, pair)):
             plane = 2 * pair + odd
             for block in range(blocks):
-                total = grad[plane, block, 2 * border : 2 * border + height]
+                total = with_rows(
+                    even_row, grad[plane, block, pl.ds(border + most, height), :], row_one[plane, block]
+                )
                 if block == 0:
                     total = total + first
                 if block == blocks - 1:
                     total = total + last
                 whole[plane, :, block * LANES : (block + 1) * LANES] = total
-            span = pl.ds(border, height)
+            span = pl.ds(most, height)
             copies.append(pltpu.make_async_copy(whole.at[plane], out.at[plane, span], sem.at[plane]))
             copies[-1].start()
-    for copy in copies:
-        copy.wait()
-
-
-def final_kernel(ncols, nrows, grad, row_one, row_two, end_one, end_two, begun, out, whole, sem):
+    return copies
+
+
+def rest_kernel(ncols, nrows, grad, row_two, end_one, end_two, out, whole, sem):
     blocks, border = row_two.shape[1:3]
     rows = grad.shape[2] - 2 * border
-    even_row, inner = sides("row", nrows)
+    _, inner, _, rest = row_parts(nrows, rows, border)
     copies = []
     for pair in range(2):
         for odd, (first, last) in enumerate(column_sums(ncols, border, end_one, end_two, pair)):
             plane = 2 * pair + odd
             for block in range(blocks):
-                came = ends(even_row, inner, row_one[plane, block], row_two[plane, block])
-                for number, at in enumerate((border, rows)):
-                    span = slice(number * border, (number + 1) * border)
-                    total = grad[plane, block, at : at + border] + came[number]
-                    if block == 0:
-                        total = total + first[span]
-                    if block == blocks - 1:
-                        total = total + last[span]
-                    whole[plane, span, block * LANES : (block + 1) * LANES] = total
-            for number, at in enumerate((0, rows - border)):
-                source = whole.at[plane, pl.ds(number * border, border)]
-                copies.append(
-                    pltpu.make_async_copy(source, out.at[plane, pl.ds(at, border)], sem.at[plane, number])
-                )
-                copies[-1].start()
+                total = grad[plane, block, pl.ds(border + rest, border), :]
+                total = total + jnp.where(inner, row_two[plane, block].astype(jnp.float32), 0.0)
+                if block == 0:
+                    total = total + first
+                if block == blocks - 1:
+                    total = total + last
+                whole[plane, :, block * LANES : (block + 1) * LANES] = total
+            span = pl.ds(rest, border)
+            copies.append(pltpu.make_async_copy(whole.at[plane], out.at[plane, span], sem.at[plane]))
+            copies[-1].start()
+    return copies
+
+
+def final_kernel(ncols, nrows, grad, row_one, row_two, mid_one, mid_two, end_one, end_two, out, *refs):
+    most, rest, most_sem, rest_sem = refs
+    copies = middle_kernel(ncols, nrows, grad, row_one, mid_one, mid_two, out, most, most_sem)
+    copies += rest_kernel(ncols, nrows, grad, row_two, end_one, end_two, out, rest, rest_sem)
     for copy in copies:
         copy.wait()
 
@@ -538,10 +560,10 @@
     tables = make_tables(width)
     edge_shape = bf16((4, blocks, border, LANES))
     corner_shape = bf16((4, border, LANES))
-    grad, line_one, edge_two, corner_two, mid_one, mid_two = kernel(
-        functools.partial(main_kernel, BATCH, ncols, nrows),
+    grad, line_one, edge_two, corner_two = kernel(
+        functools.partial(main_kernel, BATCH, nrows),
         [anywhere] * 4,
-        [whole, line_shape, edge_shape, corner_shape] + [bf16((2, rows - 2 * border, LANES))] * 2,
+        [whole, line_shape, edge_shape, corner_shape],
         "gradients",
         [
             pltpu.VMEM(tables.shape, jnp.bfloat16),
@@ -556,31 +578,34 @@
         MAIN_BYTES,
     )(tables, probe, msgs, ext)
 
-    corner_two, line_one = swap(corner_two, row_two), swap(line_one, row_one)
+    line_one, corner_two = swap(line_one, row_one), swap(corner_two, row_two)
+    mid_one, mid_two = kernel(
+        functools.partial(most_kernel, ncols, nrows), 2, [bf16((2, rows - border, LANES))] * 2, "most"
+    )(grad, line_one)
+    mid_one, mid_two, edge_two = lax.optimization_barrier((mid_one, mid_two, edge_two))
     mid_one, mid_two = swap(mid_one, col_one), swap(mid_two, col_two)
     edge_two = swap(edge_two, row_two)
     end_one, end_two = kernel(
-        functools.partial(sides_kernel, ncols, nrows), 3, [bf16((2, 2 * border, LANES))] * 2, "sides", cost=pl.CostEstimate(flops=10**10, bytes_accessed=10**6, transcendentals=0)
-    )(grad, line_one, corner_two)
+        functools.partial(sides_kernel, ncols, nrows),
+        2,
+        [bf16((2, border, LANES))] * 2,
+        "sides",
+        cost=pl.CostEstimate(flops=10**10, bytes_accessed=10**6, transcendentals=0),
+    )(grad, corner_two)
     end_one, end_two = swap(end_one, col_one), swap(end_two, col_two)
-    whole_shape = f32((4, rows, cols))
-    (out,) = kernel(
-        functools.partial(middle_kernel, ncols),
-        3,
-        [whole_shape],
-        "middle",
-        [pltpu.VMEM((4, rows - 2 * border, cols), jnp.float32), pltpu.SemaphoreType.DMA((4,))],
-        to=anywhere,
-    )(grad, mid_one, mid_two)
     (out,) = kernel(
         functools.partial(final_kernel, ncols, nrows),
-        [vmem] * 5 + [anywhere],
-        [whole_shape],
+        7,
+        [f32((4, rows, cols))],
         "final",
-        [pltpu.VMEM((4, 2 * border, cols), jnp.float32), pltpu.SemaphoreType.DMA((4, 2))],
+        [
+            pltpu.VMEM((4, rows - border, cols), jnp.float32),
+            pltpu.VMEM((4, border, cols), jnp.float32),
+            pltpu.SemaphoreType.DMA((4,)),
+            pltpu.SemaphoreType.DMA((4,)),
+        ],
         to=anywhere,
-        alias={5: 0},
-    )(grad, line_one, edge_two, end_one, end_two, out)
+    )(grad, line_one, edge_two, mid_one, mid_two, end_one, end_two)
     return out.reshape(objects.shape)
 
 

time: 43.7 us -> 44 us (level)
  the two profiles are of different devices: /device:TPU:13 before, /device:TPU:0 now
where the time goes in v3:
time: 44 us; the launch traced here: 43.6 us
  starting transfers between devices  18.9 us (43%)
  waiting for transfers between devices  14.6 us (33%)
  Pallas kernels  8.54 us (19%)
  local copies, waits for them, and re-layouts  1.44 us (3%)
    ppermute x11, starting transfers between devices, swap(): return lax.ppermute(array, ('row', 'col'), flat)  12.6 us
    ppermute x11, waiting for transfers between devices, swap(): return lax.ppermute(array, ('row', 'col'), flat)  8.43 us
    all_to_all x1, starting transfers between devices, local(): msgs = lax.all_to_all(msgs, 'col', 0, 0)  6.34 us
    all_to_all x1, waiting for transfers between devices, local(): msgs = lax.all_to_all(msgs, 'col', 0, 0)  6.16 us
    pallas_call x1, Pallas kernels, local(): kernel(functools.partial(main_kernel, BATCH, nrows), [anywhere] * 4, [who...  4.49 us
    pallas_call x1, Pallas kernels, local(): kernel(functools.partial(pack_kernel, ways, ncols), [anywhere] * 5, [side...  2.29 us
    unnamed x8, local copies, waits for them, and re-layouts  1.44 us
    pallas_call x1, Pallas kernels, local(): kernel(functools.partial(final_kernel, ncols, nrows), 7, [f32((4, rows, c...  1.19 us
  transfers between devices with their start and end apart: 12, of which 4 were waited for; matrix products, arithmetic and copies ran while one was open for 0% of the time, Pallas kernels for 1%

profile of v3, /device:TPU:0, one launch (start us, length us, event | category | flops | bytes accessed | tf_op | source)
XLA Modules:
  0.0 43.6 jit_solution(654445000321093465)
XLA Ops:
  0.0 0.0 copy-start.1
  0.0 2.3 %pack.1 = (bf16[2,256,128]{2,1,0:T(8,128)(2,1)}, bf16[2,256,128]{2,1,0:T(8,128)(2,1)}, bf16[8,272,128]{2,1,0:T(8,128)(2,1)}) custom-call(bf16[1,1,6,128,128]{4,3,2,1,0:T(8,128)(2,1)} %amps.1, s32[1,1,6]{2,1,0:T(1,128)} %owners.1, s32[1,1,6]{2,1,0:T(1,128)} %at_rows.1, s32[1,1,6]{2,1,0:T(1,128)} %at_cols.1, f32[2,2,256,256]{3,2,1,0:T(8,128)} %obj.1), custom_call_target="tpu_custom_call" | custom-call | tf_op jit(solution)/shard_map/pack/pallas_call | solution.py:525
  2.3 3.0 %collective-permute-start = (bf16[2,256,128]{2,1,0:T(8,128)(2,1)}, bf16[2,256,128]{2,1,0:T(8,128)(2,1)S(1)}, u32[]{:S(2)}, u32[]{:S(2)}) collective-permute-start(bf16[2,256,128]{2,1,0:T(8,128)(2,1)} %get-tuple-element.23), channel_id=1, source_target_pairs={{0,1},{1,0},{2,3},{3,2},{4,5},{5,4},{6,7},{7,6},{8,9},{9,8},{10,11... | collective-permute-start | bytes 393224 | tf_op jit(solution)/shard_map/ppermute | solution.py:513
  5.3 0.0 collective-permute-start.1
  5.3 6.3 %all-to-all-start = ((bf16[8,272,128]{2,1,0:T(8,128)(2,1)}), bf16[8,272,128]{2,1,0:T(8,128)(2,1)}, u32[]{:S(2)}, u32[]{:S(2)}) async-start(bf16[8,272,128]{2,1,0:T(8,128)(2,1)} %get-tuple-element.22), calls=%async_computation | async-start | bytes 1114112 | tf_op jit(solution)/shard_map/all_to_all | solution.py:544
  11.6 0.0 collective-permute-done.came_one
  11.7 0.0 collective-permute-done.1.came_two
  11.7 0.0 copy-done.1
  11.7 0.2 rows.1
  11.9 0.0 copy-start.2
  11.9 0.0 copy-start.3
  11.9 0.1 collective-permute-start.2
  12.0 1.6 %collective-permute-start.3 = (bf16[4,3,64,128]{3,2,1,0:T(8,128)(2,1)S(1)}, bf16[4,3,64,128]{3,2,1,0:T(8,128)(2,1)S(1)}, u32[]{:S(2)}, u32[]{:S(2)}) collective-permute-start(bf16[4,3,64,128]{3,2,1,0:T(8,128)(2,1)S(1)} %get-tuple-element.27), channel_id=1, source_target_pairs={{0,24},{1,25},{2,26},{3,27},{4,28},{5,29},{6,30},{7,31},{8,16},{9,... | collective-permute-start | bytes 589832 | tf_op jit(solution)/shard_map/ppermute | solution.py:513
  13.6 0.0 collective-permute-done.2.row_one
  13.6 5.1 %collective-permute-done.3.row_two = bf16[4,3,64,128]{3,2,1,0:T(8,128)(2,1)S(1)} collective-permute-done((bf16[4,3,64,128]{3,2,1,0:T(8,128)(2,1)S(1)}, bf16[4,3,64,128]{3,2,1,0:T(8,128)(2,1)S(1)}, u32[]{:S(2)}, u32[]{:S(2)}) %collective-permute-start.3) | collective-permute-done | bytes 196640 | tf_op jit(solution)/shard_map/ppermute | solution.py:513
  18.7 0.2 extend.1.refs_3_
  18.8 0.0 copy-start
  18.8 1.4 %copy-done = f32[4,3,384,128]{3,2,1,0:T(8,128)} copy-done((f32[4,3,384,128]{3,2,1,0:T(8,128)}, f32[4,3,384,128]{3,2,1,0:T(8,128)S(1)}, u32[]{:S(2)}) %copy-start) | copy-done | bytes 2359320
  20.3 6.2 %all-to-all-done.refs_2_ = bf16[8,272,128]{2,1,0:T(8,128)(2,1)} async-done(((bf16[8,272,128]{2,1,0:T(8,128)(2,1)}), bf16[8,272,128]{2,1,0:T(8,128)(2,1)}, u32[]{:S(2)}, u32[]{:S(2)}) %all-to-all-start) | async-done | bytes 557088 | tf_op jit(solution)/shard_map/all_to_all | solution.py:544
  26.4 0.0 copy-done.2
  26.4 0.0 copy-done.3
  26.4 4.5 %gradients.1 = (f32[4,3,384,128]{3,2,1,0:T(8,128)S(1)}, bf16[4,3,64,128]{3,2,1,0:T(8,128)(2,1)S(1)}, bf16[4,2,64,128]{3,2,1,0:T(8,128)(2,1)S(1)}, bf16[4,64,128]{2,1,0:T(8,128)(2,1)S(1)}) custom-call(bf16[4,256,256]{2,1,0:T(8,128)(2,1)S(1)} %copy-done.2, f32[2,2,128,128]{3,2,1,0:T(8,128)S(1)} %copy-done.3, bf16[8,272,128]{2,1,0:T(8,128)(2,1)} %all-to-all-done.refs_2_, ...), custom_call_target="tpu_custom_call" | custom-call | tf_op jit(solution)/shard_map/gradients/pallas_call | solution.py:563
  30.9 0.8 %collective-permute-start.4 = (bf16[4,3,64,128]{3,2,1,0:T(8,128)(2,1)S(1)}, bf16[4,3,64,128]{3,2,1,0:T(8,128)(2,1)S(1)}, u32[]{:S(2)}, u32[]{:S(2)}) collective-permute-start(bf16[4,3,64,128]{3,2,1,0:T(8,128)(2,1)S(1)} %get-tuple-element.29), channel_id=1, source_target_pairs={{0,8},{1,9},{2,10},{3,11},{4,12},{5,13},{6,14},{7,15},{8,0},{9,1},... | collective-permute-start | bytes 589832 | tf_op jit(solution)/shard_map/ppermute | solution.py:513
  31.7 0.9 %collective-permute-start.8 = (bf16[4,64,128]{2,1,0:T(8,128)(2,1)S(1)}, bf16[4,64,128]{2,1,0:T(8,128)(2,1)S(1)}, u32[]{:S(2)}, u32[]{:S(2)}) collective-permute-start(bf16[4,64,128]{2,1,0:T(8,128)(2,1)S(1)} %get-tuple-element.36), channel_id=1, source_target_pairs={{0,24},{1,25},{2,26},{3,27},{4,28},{5,29},{6,30},{7,31},{8,16},{9,... | collective-permute-start | bytes 196616 | tf_op jit(solution)/shard_map/ppermute | solution.py:513
  32.6 0.2 collective-permute-done.4.row_one
  32.8 0.1 most.1
  32.9 4.0 %collective-permute-start.6 = (bf16[2,192,128]{2,1,0:T(8,128)(2,1)S(1)}, bf16[2,192,128]{2,1,0:T(8,128)(2,1)S(1)}, u32[]{:S(2)}, u32[]{:S(2)}) collective-permute-start(bf16[2,192,128]{2,1,0:T(8,128)(2,1)S(1)} %get-tuple-element.34), channel_id=1, source_target_pairs={{0,1},{1,0},{2,3},{3,2},{4,5},{5,4},{6,7},{7,6},{8,9},{9,8},{10,11... | collective-permute-start | bytes 294920 | tf_op jit(solution)/shard_map/ppermute | solution.py:513
  36.9 0.0 collective-permute-start.7
  36.9 1.4 %collective-permute-start.5 = (bf16[4,2,64,128]{3,2,1,0:T(8,128)(2,1)S(1)}, bf16[4,2,64,128]{3,2,1,0:T(8,128)(2,1)S(1)}, u32[]{:S(2)}, u32[]{:S(2)}) collective-permute-start(bf16[4,2,64,128]{3,2,1,0:T(8,128)(2,1)S(1)} %get-tuple-element.33), channel_id=1, source_target_pairs={{0,24},{1,25},{2,26},{3,27},{4,28},{5,29},{6,30},{7,31},{8,16},{9,... | collective-permute-start | bytes 393224 | tf_op jit(solution)/shard_map/ppermute | solution.py:513
  38.3 0.0 collective-permute-done.8.corner_two
  38.3 0.1 sides.1
  38.4 0.8 %collective-permute-start.9 = (bf16[2,64,128]{2,1,0:T(8,128)(2,1)S(1)}, bf16[2,64,128]{2,1,0:T(8,128)(2,1)S(1)}, u32[]{:S(2)}, u32[]{:S(2)}) collective-permute-start(bf16[2,64,128]{2,1,0:T(8,128)(2,1)S(1)} %get-tuple-element.37), channel_id=1, source_target_pairs={{0,1},{1,0},{2,3},{3,2},{4,5},{5,4},{6,7},{7,6},{8,9},{9,8},{10,11... | collective-permute-start | bytes 98312 | tf_op jit(solution)/shard_map/ppermute | solution.py:513
  39.2 0.0 collective-permute-start.10
  39.2 3.2 %collective-permute-done.9.end_one = bf16[2,64,128]{2,1,0:T(8,128)(2,1)S(1)} collective-permute-done((bf16[2,64,128]{2,1,0:T(8,128)(2,1)S(1)}, bf16[2,64,128]{2,1,0:T(8,128)(2,1)S(1)}, u32[]{:S(2)}, u32[]{:S(2)}) %collective-permute-start.9) | collective-permute-done | bytes 32800 | tf_op jit(solution)/shard_map/ppermute | solution.py:513
  42.4 0.0 collective-permute-done.10.end_two
  42.4 0.0 collective-permute-done.6.mid_one
  42.4 0.0 collective-permute-done.7.mid_two
  42.4 0.0 collective-permute-done.5.row_two
  42.4 1.2 %final.1 = f32[4,256,256]{2,1,0:T(8,128)} custom-call(f32[4,3,384,128]{3,2,1,0:T(8,128)S(1)} %get-tuple-element.28.grad, bf16[4,3,64,128]{3,2,1,0:T(8,128)(2,1)S(1)} %collective-permute-done.4.row_one, bf16[4,2,64,128]{3,2,1,0:T(8,128)(2,1)S(1)} %collective-permute-done.5.row_two, bf16[2,192,128]{2,1,0:T(8,128)(2,1)S(1)} %collective-permute-done.6.mid_one, ...), custom_call_target="tpu_custom_call" | custom-call | tf_op jit(solution)/shard_map/final/pallas_call | solution.py:596
Async XLA Ops:
  0.0 11.7 %copy-start.1 = (f32[2,2,256,256]{3,2,1,0:T(8,128)S(1)}, f32[2,2,256,256]{3,2,1,0:T(8,128)}, u32[]{:S(2)}) copy-start(f32[2,2,256,256]{3,2,1,0:T(8,128)} %obj.1) | copy-start | bytes 3145732
  2.3 9.3 %collective-permute-start = (bf16[2,256,128]{2,1,0:T(8,128)(2,1)}, bf16[2,256,128]{2,1,0:T(8,128)(2,1)S(1)}, u32[]{:S(2)}, u32[]{:S(2)}) collective-permute-start(bf16[2,256,128]{2,1,0:T(8,128)(2,1)} %get-tuple-element.23), channel_id=1, source_target_pairs={{0,1},{1,0},{2,3},{3,2},{4,5},{5,4},{6,7},{7,6},{8,9},{9,8},{10,11... | collective-permute-start | bytes 393224 | tf_op jit(solution)/shard_map/ppermute | solution.py:513
  5.3 6.3 %collective-permute-start.1 = (bf16[2,256,128]{2,1,0:T(8,128)(2,1)}, bf16[2,256,128]{2,1,0:T(8,128)(2,1)S(1)}, u32[]{:S(2)}, u32[]{:S(2)}) collective-permute-start(bf16[2,256,128]{2,1,0:T(8,128)(2,1)} %get-tuple-element.24), channel_id=1, source_target_pairs={{0,8},{8,0},{16,24},{24,16},{1,2},{9,10},{17,18},{25,26},{2,1},{10... | collective-permute-start | bytes 393224 | tf_op jit(solution)/shard_map/ppermute | solution.py:513
  5.3 21.1 %all-to-all-start = ((bf16[8,272,128]{2,1,0:T(8,128)(2,1)}), bf16[8,272,128]{2,1,0:T(8,128)(2,1)}, u32[]{:S(2)}, u32[]{:S(2)}) async-start(bf16[8,272,128]{2,1,0:T(8,128)(2,1)} %get-tuple-element.22), calls=%async_computation | async-start | bytes 1114112 | tf_op jit(solution)/shard_map/all_to_all | solution.py:544
  11.9 14.6 %copy-start.2 = (bf16[4,256,256]{2,1,0:T(8,128)(2,1)S(1)}, bf16[4,256,256]{2,1,0:T(8,128)(2,1)}, u32[]{:S(2)}) copy-start(bf16[4,256,256]{2,1,0:T(8,128)(2,1)} %constant.2.clone.refs_0_) | copy-start | bytes 1572868
  11.9 14.5 %copy-start.3 = (f32[2,2,128,128]{3,2,1,0:T(8,128)S(1)}, f32[2,2,128,128]{3,2,1,0:T(8,128)}, u32[]{:S(2)}) copy-start(f32[2,2,128,128]{3,2,1,0:T(8,128)} %refs_1_.1) | copy-start | bytes 786436
  11.9 1.7 %collective-permute-start.2 = (bf16[4,3,64,128]{3,2,1,0:T(8,128)(2,1)S(1)}, bf16[4,3,64,128]{3,2,1,0:T(8,128)(2,1)S(1)}, u32[]{:S(2)}, u32[]{:S(2)}) collective-permute-start(bf16[4,3,64,128]{3,2,1,0:T(8,128)(2,1)S(1)} %get-tuple-element.26), channel_id=1, source_target_pairs={{0,8},{1,9},{2,10},{3,11},{4,12},{5,13},{6,14},{7,15},{8,0},{9,1},... | collective-permute-start | bytes 589832 | tf_op jit(solution)/shard_map/ppermute | solution.py:513
  12.0 6.7 %collective-permute-start.3 = (bf16[4,3,64,128]{3,2,1,0:T(8,128)(2,1)S(1)}, bf16[4,3,64,128]{3,2,1,0:T(8,128)(2,1)S(1)}, u32[]{:S(2)}, u32[]{:S(2)}) collective-permute-start(bf16[4,3,64,128]{3,2,1,0:T(8,128)(2,1)S(1)} %get-tuple-element.27), channel_id=1, source_target_pairs={{0,24},{1,25},{2,26},{3,27},{4,28},{5,29},{6,30},{7,31},{8,16},{9,... | collective-permute-start | bytes 589832 | tf_op jit(solution)/shard_map/ppermute | solution.py:513
  18.8 1.4 %copy-start = (f32[4,3,384,128]{3,2,1,0:T(8,128)}, f32[4,3,384,128]{3,2,1,0:T(8,128)S(1)}, u32[]{:S(2)}) copy-start(f32[4,3,384,128]{3,2,1,0:T(8,128)S(1)} %extend.1.refs_3_) | copy-start | bytes 7077892
  30.9 1.9 %collective-permute-start.4 = (bf16[4,3,64,128]{3,2,1,0:T(8,128)(2,1)S(1)}, bf16[4,3,64,128]{3,2,1,0:T(8,128)(2,1)S(1)}, u32[]{:S(2)}, u32[]{:S(2)}) collective-permute-start(bf16[4,3,64,128]{3,2,1,0:T(8,128)(2,1)S(1)} %get-tuple-element.29), channel_id=1, source_target_pairs={{0,8},{1,9},{2,10},{3,11},{4,12},{5,13},{6,14},{7,15},{8,0},{9,1},... | collective-permute-start | bytes 589832 | tf_op jit(solution)/shard_map/ppermute | solution.py:513
  31.7 6.6 %collective-permute-start.8 = (bf16[4,64,128]{2,1,0:T(8,128)(2,1)S(1)}, bf16[4,64,128]{2,1,0:T(8,128)(2,1)S(1)}, u32[]{:S(2)}, u32[]{:S(2)}) collective-permute-start(bf16[4,64,128]{2,1,0:T(8,128)(2,1)S(1)} %get-tuple-element.36), channel_id=1, source_target_pairs={{0,24},{1,25},{2,26},{3,27},{4,28},{5,29},{6,30},{7,31},{8,16},{9,... | collective-permute-start | bytes 196616 | tf_op jit(solution)/shard_map/ppermute | solution.py:513
  32.9 9.5 %collective-permute-start.6 = (bf16[2,192,128]{2,1,0:T(8,128)(2,1)S(1)}, bf16[2,192,128]{2,1,0:T(8,128)(2,1)S(1)}, u32[]{:S(2)}, u32[]{:S(2)}) collective-permute-start(bf16[2,192,128]{2,1,0:T(8,128)(2,1)S(1)} %get-tuple-element.34), channel_id=1, source_target_pairs={{0,1},{1,0},{2,3},{3,2},{4,5},{5,4},{6,7},{7,6},{8,9},{9,8},{10,11... | collective-permute-start | bytes 294920 | tf_op jit(solution)/shard_map/ppermute | solution.py:513
  36.9 5.5 %collective-permute-start.7 = (bf16[2,192,128]{2,1,0:T(8,128)(2,1)S(1)}, bf16[2,192,128]{2,1,0:T(8,128)(2,1)S(1)}, u32[]{:S(2)}, u32[]{:S(2)}) collective-permute-start(bf16[2,192,128]{2,1,0:T(8,128)(2,1)S(1)} %get-tuple-element.35), channel_id=1, source_target_pairs={{0,8},{8,0},{16,24},{24,16},{1,2},{9,10},{17,18},{25,26},{2,1},{10... | collective-permute-start | bytes 294920 | tf_op jit(solution)/shard_map/ppermute | solution.py:513
  36.9 5.5 %collective-permute-start.5 = (bf16[4,2,64,128]{3,2,1,0:T(8,128)(2,1)S(1)}, bf16[4,2,64,128]{3,2,1,0:T(8,128)(2,1)S(1)}, u32[]{:S(2)}, u32[]{:S(2)}) collective-permute-start(bf16[4,2,64,128]{3,2,1,0:T(8,128)(2,1)S(1)} %get-tuple-element.33), channel_id=1, source_target_pairs={{0,24},{1,25},{2,26},{3,27},{4,28},{5,29},{6,30},{7,31},{8,16},{9,... | collective-permute-start | bytes 393224 | tf_op jit(solution)/shard_map/ppermute | solution.py:513
  38.4 4.0 %collective-permute-start.9 = (bf16[2,64,128]{2,1,0:T(8,128)(2,1)S(1)}, bf16[2,64,128]{2,1,0:T(8,128)(2,1)S(1)}, u32[]{:S(2)}, u32[]{:S(2)}) collective-permute-start(bf16[2,64,128]{2,1,0:T(8,128)(2,1)S(1)} %get-tuple-element.37), channel_id=1, source_target_pairs={{0,1},{1,0},{2,3},{3,2},{4,5},{5,4},{6,7},{7,6},{8,9},{9,8},{10,11... | collective-permute-start | bytes 98312 | tf_op jit(solution)/shard_map/ppermute | solution.py:513
  39.2 3.2 %collective-permute-start.10 = (bf16[2,64,128]{2,1,0:T(8,128)(2,1)S(1)}, bf16[2,64,128]{2,1,0:T(8,128)(2,1)S(1)}, u32[]{:S(2)}, u32[]{:S(2)}) collective-permute-start(bf16[2,64,128]{2,1,0:T(8,128)(2,1)S(1)} %get-tuple-element.38), channel_id=1, source_target_pairs={{0,8},{8,0},{16,24},{24,16},{1,2},{9,10},{17,18},{25,26},{2,1},{10... | collective-permute-start | bytes 98312 | tf_op jit(solution)/shard_map/ppermute | solution.py:513
